TPU v7x, 512 devices: a whole 4x8x8 slice. The times are simulated.
512 devices in a mesh: ctx: 64 (over x, y, core), head: 8 (over z).
Axes of the slice: x: 4, y: 8, z: 8, core: 2. Of those that a mesh axis runs over, the one named last changes fastest.
Arguments:
- queries: bfloat16 [32768, 5120], P('ctx', 'head'), may hold values from -6 to 6
- keys: bfloat16 [32768, 1024], P('ctx', 'head'), may hold values from -6 to 6
- values: bfloat16 [32768, 1024], P('ctx', 'head'), may hold values from -6 to 6
- kept: int32 [64, 32], P('ctx'), may hold values from 0 to 511
Outputs:
- attended: bfloat16 [32768, 5120], P(('ctx', 'head'))
All inputs are finite; a program needn't handle non-finite values.
Results may differ from a plain program's by a relative error of at most 0.0033.
Values may be sent and summed in bfloat16 or wider, within the bound.
No kernel may reach another device: no remote copies, remote signals or barrier semaphores. Data moves between devices by JAX's collectives and lax.ppermute only.
A program may use at most 64 MiB of HBM per device.

v0:
```python
import math

import jax
import jax.numpy as jnp
from jax import lax
from jax.sharding import PartitionSpec as P

HD = 128
ANCHOR = 128
PASS = 32


def from_root(block, axis, source):
    block = jnp.where(lax.axis_index(axis) == source, block, jnp.zeros_like(block))
    return lax.psum(block, axis)


def head_outputs(grouped, key_rows, value_rows, key_mask, deliver):
    group_size = grouped.shape[2]
    head_size = grouped.shape[3]
    scale = 1.0 / math.sqrt(head_size)
    results = []
    for group_index in range(group_size):
        query_rows = grouped[:, 0, group_index, :]
        scores = (
            jnp.einsum("rd,sd->rs", query_rows, key_rows, preferred_element_type=jnp.float32)
            * scale
        )
        masked = jnp.where(key_mask, scores, -1e30)
        largest = jnp.max(masked, axis=1)
        weights = jnp.where(key_mask, jnp.exp(masked - largest[:, None]), 0.0)
        totals = jnp.sum(weights, axis=1)
        mixed = jnp.dot(
            weights.astype(jnp.bfloat16), value_rows, preferred_element_type=jnp.float32
        )
        finished = (mixed / totals[:, None]).astype(jnp.bfloat16)
        results.append(deliver(finished))
    return results


def body(queries, keys, values, kept):
    row_count = queries.shape[0]
    local_heads = keys.shape[1] // HD
    group_size = queries.shape[1] // keys.shape[1]
    host_index = lax.axis_index("ctx")
    grouped = queries.reshape(row_count, local_heads, group_size, HD)
    anchor = from_root(jnp.stack([keys[:ANCHOR], values[:ANCHOR]]), "ctx", 0)
    picked_keys = keys[kept[0]]
    picked_values = values[kept[0]]
    positions = jnp.arange(row_count, dtype=jnp.int32)
    causal = positions[None, :] <= positions[:, None]
    anchor_mask = jnp.broadcast_to(host_index > 0, (row_count, ANCHOR))
    far_keys, far_values = (
        lax.all_gather(picked_keys, "ctx", axis=0, tiled=True),
        lax.all_gather(picked_values, "ctx", axis=0, tiled=True),
    )
    owners = jnp.arange(far_keys.shape[0], dtype=jnp.int32) // PASS
    far_mask = jnp.broadcast_to((owners < host_index)[None, :], (row_count, far_keys.shape[0]))
    key_rows = jnp.concatenate([anchor[0], far_keys, keys], 0)
    value_rows = jnp.concatenate([anchor[1], far_values, values], 0)
    key_mask = jnp.concatenate([anchor_mask, far_mask, causal], 1)

    def deliver(finished):
        return finished

    pieces = head_outputs(grouped, key_rows, value_rows, key_mask, deliver)
    attended = jnp.concatenate(pieces, 1)
    return lax.all_to_all(attended, "head", split_axis=0, concat_axis=1, tiled=True)


def solution(mesh):
    return jax.shard_map(
        body,
        mesh=mesh,
        in_specs=(P("ctx", "head"), P("ctx", "head"), P("ctx", "head"), P("ctx", None)),
        out_specs=P(("ctx", "head"), None),
        check_vma=False,
    )
```

profile of v0, /device:TPU:6, one launch (start us, length us, event | category | flops | bytes accessed | tf_op | source)
XLA Modules:
  0.0 249.1 jit_solution(17877526814326177472)
XLA Ops:
  6.5 0.0 copy-start
  6.5 0.0 all-reduce.2.cloned.1.call-start
  6.5 0.8 slice_bitcast_fusion.12
  7.3 0.8 slice_bitcast_fusion.13
  8.1 0.6 maximum_select_fusion
  8.7 0.0 all-reduce.2.cloned.1.call-update
  8.8 0.1 iota_compare_fusion
  8.9 0.7 fusion.79
  9.5 1.5 gather_fusion
  11.0 1.5 gather_fusion.1
  12.5 52.8 %all-gather = bf16[2048,128]{1,0:T(8,128)(2,1)S(1)} all-gather(bf16[32,128]{1,0:T(8,128)(2,1)S(1)} %gather_fusion), channel_id=2, replica_groups=mesh['ctx'=64,'head'=8] {'ctx'}, dimensions={0}, use_global_device_ids=true | all-gather | bytes 532480 | tf_op jit(solution)/shard_map/all_gather | solution.py:54
  65.3 47.3 %all-gather.1 = bf16[2048,128]{1,0:T(8,128)(2,1)S(1)} all-gather(bf16[32,128]{1,0:T(8,128)(2,1)S(1)} %gather_fusion.1), channel_id=3, replica_groups=mesh['ctx'=64,'head'=8] {'ctx'}, dimensions={0}, use_global_device_ids=true | all-gather | bytes 532480 | tf_op jit(solution)/shard_map/all_gather | solution.py:55
  112.6 1.3 copy.13
  114.0 80.3 %all-reduce.2.cloned.1.call-done = bf16[2,128,128]{2,1,0:T(8,128)(2,1)} async-done(((bf16[2,128,128]{2,1,0:T(8,128)(2,1)}), bf16[2,128,128]{2,1,0:T(8,128)(2,1)}) %all-reduce.2.cloned.1.call-update) | async-done | bytes 65552 | tf_op jit(solution)/shard_map/psum | solution.py:15
  194.3 0.8 slice_bitcast_fusion.10
  195.1 0.0 copy-done
  195.1 0.9 fusion.86
  196.0 1.0 fusion.87
  197.0 1.0 fusion.88
  197.9 1.0 fusion.89
  198.9 1.0 fusion.85
  199.9 0.0 copy-start.1
  199.9 7.3 %fusion.8 = (f32[512]{0:T(512)S(1)}, f32[512]{0:T(512)S(1)}, f32[512]{0:T(512)S(1)}, f32[512]{0:T(512)S(1)}, f32[512]{0:T(512)S(1)}) fusion(f32[512,2688]{0,1:T(8,128)S(1)} %get-tuple-element.15, f32[512]{0:T(512)S(1)} %get-tuple-element.14, pred[512,512]{0,1:T(32,128)(4,1)S(1)} %iota_compare_fusion, pred[2688]{0:T(1024)(128)(4,1)S(1)} %pad_add_fusion.1, ...), kind=kLoop, calls=%fused_computation.21 | loop fusion | flops 22017536 | bytes 27810432 | tf_op jit(solution)/shard_map/reduce_sum | solution.py:32
  207.2 0.0 copy-done.1
  207.2 1.3 fusion.36
  208.5 1.3 fusion.45
  209.7 1.3 fusion.54
  211.0 1.3 fusion.63
  212.3 1.3 fusion.72
  213.5 0.3 copy.19
  213.8 27.6 %all_to_all.19 = bf16[8,64,640]{2,1,0:T(8,128)(2,1)S(1)} all-to-all(bf16[8,64,640]{2,1,0:T(8,128)(2,1)S(1)} %bitcast.57), channel_id=1, replica_groups=mesh['ctx'=64,'head'=8] {'head'}, dimensions={0} | all-to-all | bytes 1310720 | tf_op jit(solution)/shard_map/all_to_all | solution.py:68
  241.4 0.9 copy.21
  (4 shorter events, 0.0 us)
Async XLA Ops:
  6.5 188.5 %copy-start = (bf16[512,128]{1,0:T(8,128)(2,1)S(1)}, bf16[512,128]{1,0:T(8,128)(2,1)}, u32[]{:S(2)}) copy-start(bf16[512,128]{1,0:T(8,128)(2,1)} %param.5) | copy-start | bytes 393220
  6.5 187.8 %all-reduce.2.cloned.1.call-start = ((), (), s32[]{:S(2)}) async-start(), calls=%async_computation.1 | async-start | bytes 131072 | tf_op jit(solution)/shard_map/psum | solution.py:15
  199.9 7.3 %copy-start.1 = (bf16[512,128]{1,0:T(8,128)(2,1)S(1)}, bf16[512,128]{1,0:T(8,128)(2,1)}, u32[]{:S(2)}) copy-start(bf16[512,128]{1,0:T(8,128)(2,1)} %param.6) | copy-start | bytes 393220
Sparse Core Ops, SparseCore 0:
  10.8 183.4 all-reduce.1
where the time goes:
time: 251 us; the launch traced here: 249 us
  blocking collectives  128 us (51%)
  waiting for transfers between devices  80.3 us (32%)
  between operations  13.5 us (5%)
  matrix products  11.1 us (4%)
  other arithmetic  8.72 us (3%)
  local copies, waits for them, and re-layouts  7.87 us (3%)
    psum x1, waiting for transfers between devices, from_root(): return lax.psum(block, axis)  80.3 us
    all_gather x1, blocking collectives, body(): lax.all_gather(picked_keys, 'ctx', axis=0, tiled=True)  52.8 us
    all_gather x1, blocking collectives, body(): lax.all_gather(picked_values, 'ctx', axis=0, tiled=True)  47.3 us
    all_to_all x1, blocking collectives, body(): lax.all_to_all(attended, 'head', split_axis=0, concat_axis=1, tiled=True)  27.6 us
    reduce_sum x1, other arithmetic, head_outputs(): totals = jnp.sum(weights, axis=1)  7.32 us
    dot_general x5, matrix products, head_outputs(): jnp.dot(weights.astype(jnp.bfloat16), value_rows, preferred_element_type=...  6.3 us
  transfers between devices with their start and end apart: 1, of which 1 were waited for; matrix products, arithmetic and copies ran while one was open for 2% of the time, Pallas kernels for 0%

commit v1 on v0

v1 whole, which is shorter than its diff:
```python
import functools
import math

import jax
import jax.numpy as jnp
from jax import lax
from jax.experimental import pallas as pl
from jax.experimental.pallas import tpu as pltpu
from jax.sharding import PartitionSpec as P

HD = 128
ANCHOR = 128
PASS = 32
NX, NY, NC = 4, 8, 2
CHIPS = NX * NY
HALF = CHIPS * PASS
FAR = ANCHOR + 2 * HALF
ROWS = 512
TILE = 256
STEP = 16
NEG = -1e30
SCALE = math.log2(math.e) / math.sqrt(HD)


def ctx_of(x, y, core):
    return (x * NY + y) * NC + core


GROUPS_XY = [[ctx_of(x, y, c) for x in range(NX) for y in range(NY)] for c in range(NC)]
PAIRS_X = [[(0, ctx_of(x, 0, 0))] for x in range(1, NX)]
PAIRS_FAR = [(ctx_of(x, 0, 0), ctx_of(x, NY // 2, 0)) for x in range(NX)]
PAIRS_NEAR = [
    [(ctx_of(x, y, 0), ctx_of(x, y + step, 0)) for x in range(NX) for y in (0, NY // 2)]
    for step in range(1, NY // 2)
]
PAIRS_UP = [(ctx_of(x, y, 0), ctx_of(x, y, 1)) for x in range(NX) for y in range(NY)]
PAIRS_CORE = [(i, i ^ 1) for i in range(NX * NY * NC)]


def pick_kernel(kept_ref, key_ref, value_ref, sent_ref, start_ref):
    row = lax.broadcasted_iota(jnp.int32, (ROWS, PASS), 0)
    chosen = jnp.where(row == kept_ref[...], 1.0, 0.0).astype(jnp.bfloat16)
    for ref, base in ((key_ref, 0), (value_ref, PASS)):
        picked = lax.dot_general(
            chosen, ref[...], (((0,), (0,)), ((), ())), preferred_element_type=jnp.float32
        ).astype(jnp.bfloat16)
        for chip in range(CHIPS):
            sent_ref[chip, base : base + PASS, :] = picked
    first = lax.axis_index("ctx") == 0
    for ref, base in ((key_ref, 0), (value_ref, ANCHOR)):
        rows = ref[:ANCHOR, :]
        start_ref[base : base + ANCHOR, :] = jnp.where(first, rows, jnp.zeros_like(rows))


def pick(kept, keys, values):
    return pl.pallas_call(
        pick_kernel,
        out_shape=[
            jax.ShapeDtypeStruct((CHIPS, 2 * PASS, HD), jnp.bfloat16),
            jax.ShapeDtypeStruct((2 * ANCHOR, HD), jnp.bfloat16),
        ],
    )(kept, keys, values)


def attention_kernel(
    heads, q_ref, mine_ref, other_ref, anchor_ref, relayed_ref, key_ref, value_ref, out_ref, kx, kt, vx, s0, s1, p0, p1
):
    me = lax.axis_index("ctx")
    core = lax.rem(me, NC)

    anchor = anchor_ref[...] + relayed_ref[...]
    kx[0:ANCHOR, :] = anchor[:ANCHOR]
    vx[0:ANCHOR, :HD] = anchor[ANCHOR:]
    for ref, base in ((mine_ref, ANCHOR), (other_ref, ANCHOR + HALF)):
        for chip in range(CHIPS):
            at = slice(base + chip * PASS, base + (chip + 1) * PASS)
            kx[at, :] = ref[chip, :PASS, :]
            vx[at, :HD] = ref[chip, PASS:, :]
    kx[FAR:, :] = key_ref[...]
    vx[FAR:, :HD] = value_ref[...]
    vx[:, HD:] = jnp.ones((FAR + ROWS, HD), jnp.bfloat16)

    for start in range(0, FAR + ROWS, HD):
        kt[:HD, start : start + HD] = kx[start : start + HD, :].T
    row = lax.broadcasted_iota(jnp.int32, (HD, HALF), 0)
    at = lax.broadcasted_iota(jnp.int32, (HD, HALF), 1)
    never = jnp.where(row == 0, NEG, 0.0)
    kt[HD:, 0:ANCHOR] = jnp.where(row[:, :ANCHOR] * 0 < me, 0.0, never[:, :ANCHOR]).astype(
        jnp.bfloat16
    )
    for owner_core, base in ((core, ANCHOR), (1 - core, ANCHOR + HALF)):
        owner = NC * (at >> 5) + owner_core
        kt[HD:, base : base + HALF] = jnp.where(owner < me, 0.0, never).astype(jnp.bfloat16)
    kt[HD:, FAR:] = jnp.zeros((HD, ROWS), jnp.bfloat16)

    lane = lax.broadcasted_iota(jnp.int32, (TILE, HD), 1)
    flag = jnp.where(lane == 0, 1.0, 0.0).astype(jnp.bfloat16)
    items = [(head, tile) for head in range(heads) for tile in range(ROWS // TILE)]
    scores, weights = (s0, s1), (p0, p1)

    def width(tile):
        return FAR + (tile + 1) * TILE

    def score_columns(index):
        head, tile = items[index]
        rows = q_ref[tile * TILE : (tile + 1) * TILE, head * HD : (head + 1) * HD]
        queries = jnp.concatenate([rows, flag], 1)
        target = scores[index % 2]
        total = width(tile)
        for start in range(0, total, TILE):
            stop = min(start + TILE, total)
            yield target, start, stop, queries

    def score(piece):
        target, start, stop, queries = piece
        target[:, start:stop] = jnp.dot(
            queries, kt[:, start:stop], preferred_element_type=jnp.float32
        )

    for piece in score_columns(0):
        score(piece)
    for index, (head, tile) in enumerate(items):
        coming = list(score_columns(index + 1)) if index + 1 < len(items) else []
        total = width(tile)
        full = total - TILE
        source, target = scores[index % 2], weights[index % 2]
        for step in range(TILE // STEP):
            if step < len(coming):
                score(coming[step])
            r0 = step * STEP
            s = source[r0 : r0 + STEP, :total]
            at = lax.broadcasted_iota(jnp.int32, (STEP, TILE), 1)
            to = lax.broadcasted_iota(jnp.int32, (STEP, TILE), 0) + r0
            s = jnp.concatenate([s[:, :full], jnp.where(at <= to, s[:, full:], NEG)], 1)
            largest = jnp.max(s, axis=1, keepdims=True)
            target[r0 : r0 + STEP, :total] = jnp.exp2((s - largest) * SCALE).astype(jnp.bfloat16)
        for piece in coming[TILE // STEP :]:
            score(piece)
        mixed = jnp.dot(target[:, :total], vx[:total, :], preferred_element_type=jnp.float32)
        out_ref[tile * TILE : (tile + 1) * TILE, head * HD : (head + 1) * HD] = (
            mixed[:, :HD] / mixed[:, HD:]
        ).astype(jnp.bfloat16)


def attention(queries, mine, other, anchor, relayed, keys, values):
    heads = queries.shape[1] // HD
    return pl.pallas_call(
        functools.partial(attention_kernel, heads),
        out_shape=jax.ShapeDtypeStruct((ROWS, heads * HD), jnp.bfloat16),
        scratch_shapes=[
            pltpu.VMEM((FAR + ROWS, HD), jnp.bfloat16),
            pltpu.VMEM((2 * HD, FAR + ROWS), jnp.bfloat16),
            pltpu.VMEM((FAR + ROWS, 2 * HD), jnp.bfloat16),
            pltpu.VMEM((TILE, FAR + ROWS), jnp.float32),
            pltpu.VMEM((TILE, FAR + ROWS), jnp.float32),
            pltpu.VMEM((TILE, FAR + ROWS), jnp.bfloat16),
            pltpu.VMEM((TILE, FAR + ROWS), jnp.bfloat16),
        ],
        compiler_params=pltpu.CompilerParams(vmem_limit_bytes=40 * 1024 * 1024),
    )(queries, mine, other, anchor, relayed, keys, values)


def body(queries, keys, values, kept):
    sent, anchor = pick(kept, keys, values)
    mine = lax.all_to_all(sent, "ctx", 0, 0, axis_index_groups=GROUPS_XY)
    anchor = sum([lax.ppermute(anchor, "ctx", pairs) for pairs in PAIRS_X], anchor)
    anchor = anchor + lax.ppermute(anchor, "ctx", PAIRS_FAR)
    anchor = sum([lax.ppermute(anchor, "ctx", pairs) for pairs in PAIRS_NEAR], anchor)
    relayed = lax.ppermute(anchor, "ctx", PAIRS_UP)
    mine, anchor, relayed = lax.optimization_barrier((mine, anchor, relayed))
    other = lax.ppermute(mine, "ctx", PAIRS_CORE)

    attended = attention(queries, mine, other, anchor, relayed, keys, values)
    return lax.all_to_all(attended, "head", split_axis=0, concat_axis=1, tiled=True)


def solution(mesh):
    return jax.shard_map(
        body,
        mesh=mesh,
        in_specs=(P("ctx", "head"), P("ctx", "head"), P("ctx", "head"), P("ctx", None)),
        out_specs=P(("ctx", "head"), None),
        check_vma=False,
    )
```

time: 251 us -> 81.1 us (0.32)
  the two profiles are of different devices: /device:TPU:6 before, /device:TPU:43 now
where the time goes in v1:
time: 81.1 us; the launch traced here: 80.7 us
  blocking collectives  30.5 us (38%)
  waiting for transfers between devices  21.2 us (26%)
  starting transfers between devices  17.5 us (22%)
  Pallas kernels  10.3 us (13%)
  local copies, waits for them, and re-layouts  0.92 us (1%)
    all_to_all x1, blocking collectives, body(): lax.all_to_all(attended, 'head', split_axis=0, concat_axis=1, tiled=True)  30.5 us
    ppermute x1, waiting for transfers between devices, body(): relayed = lax.ppermute(anchor, 'ctx', PAIRS_UP)  19.4 us
    all_to_all x1, starting transfers between devices, body(): mine = lax.all_to_all(sent, 'ctx', 0, 0, axis_index_groups=GROUPS_XY)  9.26 us
    pallas_call x1, Pallas kernels, attention(): pl.pallas_call(functools.partial(attention_kernel, heads), out_shape=jax....  8.3 us
    ppermute x6, starting transfers between devices, body(): lax.ppermute(anchor, 'ctx', pairs)  4.25 us
    ppermute x1, starting transfers between devices, body(): other = lax.ppermute(mine, 'ctx', PAIRS_CORE)  2.06 us
    pallas_call x1, Pallas kernels, pick(): pl.pallas_call(pick_kernel, out_shape=[jax.ShapeDtypeStruct((CHIPS, 2 * P...  2.03 us
    ppermute x1, waiting for transfers between devices, body(): other = lax.ppermute(mine, 'ctx', PAIRS_CORE)  1.73 us
  transfers between devices with their start and end apart: 10, of which 2 were waited for; matrix products, arithmetic and copies ran while one was open for 0% of the time, Pallas kernels for 0%

profile of v1, /device:TPU:43, one launch (start us, length us, event | category | flops | bytes accessed | tf_op | source)
XLA Modules:
  0.0 80.7 jit_solution(4068423571026291017)
XLA Ops:
  0.0 2.0 %shard_map.46 = (bf16[32,64,128]{2,1,0:T(8,128)(2,1)}, bf16[256,128]{1,0:T(8,128)(2,1)}) custom-call(s32[1,32]{1,0:T(1,128)} %kept_ref.1, bf16[512,128]{1,0:T(8,128)(2,1)} %key_ref.3, bf16[512,128]{1,0:T(8,128)(2,1)} %value_ref.3), custom_call_target="tpu_custom_call" | custom-call | tf_op jit(solution)/shard_map/pallas_call | solution.py:56
  2.0 0.0 copy-start.3
  2.0 0.0 copy-start.2
  2.0 9.3 %all-to-all-start = ((bf16[32,64,128]{2,1,0:T(8,128)(2,1)}), bf16[32,64,128]{2,1,0:T(8,128)(2,1)S(1)}, u32[]{:S(2)}, u32[]{:S(2)}) async-start(bf16[32,64,128]{2,1,0:T(8,128)(2,1)} %get-tuple-element.10), calls=%async_computation | async-start | bytes 1048576 | tf_op jit(solution)/shard_map/all_to_all | solution.py:165
  11.3 0.0 copy-start
  11.3 0.0 copy-done.3
  11.3 0.8 collective-permute-start.2
  12.1 0.7 collective-permute-start.1
  12.8 0.7 collective-permute-start
  13.5 0.0 collective-permute-done.2
  13.5 0.0 collective-permute-done.1
  13.5 0.0 collective-permute-done
  13.5 0.7 collective-permute-start.3
  14.2 0.0 collective-permute-done.3
  14.2 0.0 copy-start.1
  14.3 0.8 collective-permute-start.6
  15.1 0.7 collective-permute-start.5
  15.7 0.7 collective-permute-start.4
  16.4 0.0 collective-permute-done.6
  16.4 0.0 collective-permute-done.5
  16.4 0.0 collective-permute-done.4
  16.5 1.3 %collective-permute-start.7 = (bf16[256,128]{1,0:T(8,128)(2,1)S(1)}, bf16[256,128]{1,0:T(8,128)(2,1)S(1)}, u32[]{:S(2)}, u32[]{:S(2)}) collective-permute-start(bf16[256,128]{1,0:T(8,128)(2,1)S(1)} %add_add_fusion.anchor_ref), channel_id=1, source_target_pairs={{0,8},{16,24},{32,40},{48,56},{64,72},{80,88},{96,104},{112,120},{... | collective-permute-start | bytes 196616 | tf_op jit(solution)/shard_map/ppermute | solution.py:169
  17.8 19.4 %collective-permute-done.7.relayed_ref = bf16[256,128]{1,0:T(8,128)(2,1)S(1)} collective-permute-done((bf16[256,128]{1,0:T(8,128)(2,1)S(1)}, bf16[256,128]{1,0:T(8,128)(2,1)S(1)}, u32[]{:S(2)}, u32[]{:S(2)}) %collective-permute-start.7) | collective-permute-done | bytes 65568 | tf_op jit(solution)/shard_map/ppermute | solution.py:169
  37.2 0.0 all-to-all-done.mine_ref
  37.2 2.1 %collective-permute-start.8 = (bf16[32,64,128]{2,1,0:T(8,128)(2,1)S(1)}, bf16[32,64,128]{2,1,0:T(8,128)(2,1)S(1)}, u32[]{:S(2)}, u32[]{:S(2)}) collective-permute-start(bf16[32,64,128]{2,1,0:T(8,128)(2,1)S(1)} %all-to-all-done.mine_ref), channel_id=1, source_target_pairs={{0,8},{8,0},{16,24},{24,16},{32,40},{40,32},{48,56},{56,48},{64,72... | collective-permute-start | bytes 1572872 | tf_op jit(solution)/shard_map/ppermute | solution.py:171
  39.2 1.7 %collective-permute-done.8.other_ref = bf16[32,64,128]{2,1,0:T(8,128)(2,1)S(1)} collective-permute-done((bf16[32,64,128]{2,1,0:T(8,128)(2,1)S(1)}, bf16[32,64,128]{2,1,0:T(8,128)(2,1)S(1)}, u32[]{:S(2)}, u32[]{:S(2)}) %collective-permute-start.8) | collective-permute-done | bytes 524320 | tf_op jit(solution)/shard_map/ppermute | solution.py:171
  41.0 0.0 copy-done.2
  41.0 0.0 copy-done
  41.0 0.0 copy-done.1
  41.0 8.3 %shard_map.47 = bf16[512,640]{1,0:T(8,128)(2,1)S(1)} custom-call(bf16[512,640]{1,0:T(8,128)(2,1)S(1)} %copy-done, bf16[32,64,128]{2,1,0:T(8,128)(2,1)S(1)} %all-to-all-done.mine_ref, bf16[32,64,128]{2,1,0:T(8,128)(2,1)S(1)} %collective-permute-done.8.other_ref, bf16[256,128]{1,0:T(8,128)(2,1)S(1)} %add_add_fusion.anchor_ref, ...), custom_call_target="tpu_custom_call" | custom-call | tf_op jit(solution)/shard_map/pallas_call | solution.py:147
  49.3 30.5 %all_to_all.24 = bf16[8,64,640]{2,1,0:T(8,128)(2,1)S(1)} all-to-all(bf16[8,64,640]{2,1,0:T(8,128)(2,1)S(1)} %bitcast.4), channel_id=1, replica_groups=mesh['ctx'=64,'head'=8] {'head'}, dimensions={0} | all-to-all | bytes 1310720 | tf_op jit(solution)/shard_map/all_to_all | solution.py:174
  79.8 0.9 %copy.6 = bf16[8,8,8,640]{3,2,0,1:T(8,128)(2,1)} copy(bf16[8,8,8,640]{3,2,1,0:T(8,128)(2,1)S(1)} %bitcast.5) | data formatting | bytes 1310720 | tf_op jit(solution)/shard_map/all_to_all | solution.py:174
  (3 shorter events, 0.1 us)
Async XLA Ops:
  2.0 9.3 %copy-start.3 = (bf16[256,128]{1,0:T(8,128)(2,1)S(1)}, bf16[256,128]{1,0:T(8,128)(2,1)}, u32[]{:S(2)}) copy-start(bf16[256,128]{1,0:T(8,128)(2,1)} %get-tuple-element.11) | copy-start | bytes 196612
  2.0 38.9 %copy-start.2 = (bf16[512,128]{1,0:T(8,128)(2,1)S(1)}, bf16[512,128]{1,0:T(8,128)(2,1)}, u32[]{:S(2)}) copy-start(bf16[512,128]{1,0:T(8,128)(2,1)} %value_ref.3) | copy-start | bytes 393220
  2.0 35.1 %all-to-all-start = ((bf16[32,64,128]{2,1,0:T(8,128)(2,1)}), bf16[32,64,128]{2,1,0:T(8,128)(2,1)S(1)}, u32[]{:S(2)}, u32[]{:S(2)}) async-start(bf16[32,64,128]{2,1,0:T(8,128)(2,1)} %get-tuple-element.10), calls=%async_computation | async-start | bytes 1048576 | tf_op jit(solution)/shard_map/all_to_all | solution.py:165
  11.3 29.7 %copy-start = (bf16[512,640]{1,0:T(8,128)(2,1)S(1)}, bf16[512,640]{1,0:T(8,128)(2,1)}, u32[]{:S(2)}) copy-start(bf16[512,640]{1,0:T(8,128)(2,1)} %q_ref.1) | copy-start | bytes 1966084
  11.3 2.2 %collective-permute-start.2 = (bf16[256,128]{1,0:T(8,128)(2,1)S(1)}, bf16[256,128]{1,0:T(8,128)(2,1)S(1)}, u32[]{:S(2)}, u32[]{:S(2)}) collective-permute-start(bf16[256,128]{1,0:T(8,128)(2,1)S(1)} %copy-done.3), channel_id=1, source_target_pairs={{0,384},{1,385},{2,386},{3,387},{4,388},{5,389},{6,390},{7,391}} | collective-permute-start | bytes 196616 | tf_op jit(solution)/shard_map/ppermute | solution.py:166
  12.1 1.4 %collective-permute-start.1 = (bf16[256,128]{1,0:T(8,128)(2,1)S(1)}, bf16[256,128]{1,0:T(8,128)(2,1)S(1)}, u32[]{:S(2)}, u32[]{:S(2)}) collective-permute-start(bf16[256,128]{1,0:T(8,128)(2,1)S(1)} %copy-done.3), channel_id=1, source_target_pairs={{0,256},{1,257},{2,258},{3,259},{4,260},{5,261},{6,262},{7,263}} | collective-permute-start | bytes 196616 | tf_op jit(solution)/shard_map/ppermute | solution.py:166
  12.8 0.7 collective-permute-start
  13.5 0.7 collective-permute-start.3
  14.2 26.7 %copy-start.1 = (bf16[512,128]{1,0:T(8,128)(2,1)S(1)}, bf16[512,128]{1,0:T(8,128)(2,1)}, u32[]{:S(2)}) copy-start(bf16[512,128]{1,0:T(8,128)(2,1)} %key_ref.3) | copy-start | bytes 393220
  14.3 2.2 %collective-permute-start.6 = (bf16[256,128]{1,0:T(8,128)(2,1)S(1)}, bf16[256,128]{1,0:T(8,128)(2,1)S(1)}, u32[]{:S(2)}, u32[]{:S(2)}) collective-permute-start(bf16[256,128]{1,0:T(8,128)(2,1)S(1)} %add.24), channel_id=1, source_target_pairs={{0,48},{64,112},{128,176},{192,240},{256,304},{320,368},{384,432},... | collective-permute-start | bytes 196616 | tf_op jit(solution)/shard_map/ppermute | solution.py:168
  15.1 1.4 %collective-permute-start.5 = (bf16[256,128]{1,0:T(8,128)(2,1)S(1)}, bf16[256,128]{1,0:T(8,128)(2,1)S(1)}, u32[]{:S(2)}, u32[]{:S(2)}) collective-permute-start(bf16[256,128]{1,0:T(8,128)(2,1)S(1)} %add.24), channel_id=1, source_target_pairs={{0,32},{64,96},{128,160},{192,224},{256,288},{320,352},{384,416},{... | collective-permute-start | bytes 196616 | tf_op jit(solution)/shard_map/ppermute | solution.py:168
  15.7 0.7 collective-permute-start.4
  16.5 20.7 %collective-permute-start.7 = (bf16[256,128]{1,0:T(8,128)(2,1)S(1)}, bf16[256,128]{1,0:T(8,128)(2,1)S(1)}, u32[]{:S(2)}, u32[]{:S(2)}) collective-permute-start(bf16[256,128]{1,0:T(8,128)(2,1)S(1)} %add_add_fusion.anchor_ref), channel_id=1, source_target_pairs={{0,8},{16,24},{32,40},{48,56},{64,72},{80,88},{96,104},{112,120},{... | collective-permute-start | bytes 196616 | tf_op jit(solution)/shard_map/ppermute | solution.py:169
  37.2 3.8 %collective-permute-start.8 = (bf16[32,64,128]{2,1,0:T(8,128)(2,1)S(1)}, bf16[32,64,128]{2,1,0:T(8,128)(2,1)S(1)}, u32[]{:S(2)}, u32[]{:S(2)}) collective-permute-start(bf16[32,64,128]{2,1,0:T(8,128)(2,1)S(1)} %all-to-all-done.mine_ref), channel_id=1, source_target_pairs={{0,8},{8,0},{16,24},{24,16},{32,40},{40,32},{48,56},{56,48},{64,72... | collective-permute-start | bytes 1572872 | tf_op jit(solution)/shard_map/ppermute | solution.py:171

commit v2 on v1

v2 whole, which is shorter than its diff:
```python
import functools
import math

import jax
import jax.numpy as jnp
from jax import lax
from jax.experimental import pallas as pl
from jax.experimental.pallas import tpu as pltpu
from jax.sharding import PartitionSpec as P

HD = 128
ANCHOR = 128
PASS = 32
NX, NY, NC = 4, 8, 2
CHIPS = NX * NY
HALF = CHIPS * PASS
FAR = 2 * HALF
ROWS = 512
TILE = 256
STEP = 16
SUBLANES = 8
NEG = -1e30
SCALE = math.log2(math.e) / math.sqrt(HD)


def ctx_of(x, y, core):
    return (x * NY + y) * NC + core


GROUPS_XY = [[ctx_of(x, y, c) for x in range(NX) for y in range(NY)] for c in range(NC)]
PAIRS_UP = [(0, 1)]
PAIRS_X = [[(c, ctx_of(x, 0, c)) for c in range(NC)] for x in range(1, NX)]
PAIRS_Y = {
    step: [
        (ctx_of(x, y, c), ctx_of(x, y + step, c))
        for x in range(NX)
        for y in range(0, NY, 2 * step)
        for c in range(NC)
    ]
    for step in (4, 2, 1)
}
PAIRS_CORE = [(i, i ^ 1) for i in range(NX * NY * NC)]


def pick_kernel(kept_ref, key_ref, value_ref, sent_ref, start_ref):
    row = lax.broadcasted_iota(jnp.int32, (ROWS, PASS), 0)
    chosen = jnp.where(row == kept_ref[...], 1.0, 0.0).astype(jnp.bfloat16)
    for ref, base in ((key_ref, 0), (value_ref, PASS)):
        picked = lax.dot_general(
            chosen, ref[...], (((0,), (0,)), ((), ())), preferred_element_type=jnp.float32
        ).astype(jnp.bfloat16)
        for chip in range(CHIPS):
            sent_ref[chip, base : base + PASS, :] = picked
    first = lax.axis_index("ctx") == 0
    for ref, base in ((key_ref, 0), (value_ref, ANCHOR)):
        rows = ref[:ANCHOR, :]
        start_ref[base : base + ANCHOR, :] = jnp.where(first, rows, jnp.zeros_like(rows))


def pick(kept, keys, values):
    return pl.pallas_call(
        pick_kernel,
        out_shape=[
            jax.ShapeDtypeStruct((CHIPS, 2 * PASS, HD), jnp.bfloat16),
            jax.ShapeDtypeStruct((2 * ANCHOR, HD), jnp.bfloat16),
        ],
    )(kept, keys, values)


def attention_kernel(
    heads, q_ref, mine_ref, other_ref, key_ref, value_ref, out_ref, log_ref,
    kx, kt, mask, vx, s0, s1, p0, p1, m0, m1,
):
    me = lax.axis_index("ctx")
    core = lax.rem(me, NC)

    for ref, base in ((mine_ref, 0), (other_ref, HALF)):
        for chip in range(CHIPS):
            at = slice(base + chip * PASS, base + (chip + 1) * PASS)
            kx[at, :] = ref[chip, :PASS, :]
            vx[at, :HD] = ref[chip, PASS:, :]
    kx[FAR:, :] = key_ref[...]
    vx[FAR:, :HD] = value_ref[...]
    vx[:, HD:] = jnp.ones((FAR + ROWS, HD), jnp.bfloat16)

    for start in range(0, FAR + ROWS, HD):
        kt[:, start : start + HD] = kx[start : start + HD, :].T
    at = lax.broadcasted_iota(jnp.int32, (SUBLANES, HALF), 1)
    for owner_core, base in ((core, 0), (1 - core, HALF)):
        owner = NC * (at >> 5) + owner_core
        mask[:, base : base + HALF] = jnp.where(owner < me, 0.0, NEG)

    items = [(head, tile) for head in range(heads) for tile in range(ROWS // TILE)]
    scores, weights = (s0, s1), (p0, p1)

    causal = lax.broadcasted_iota(jnp.int32, (TILE, TILE), 1) <= lax.broadcasted_iota(
        jnp.int32, (TILE, TILE), 0
    )

    def width(tile):
        return FAR + (tile + 1) * TILE

    def pieces(index):
        cuts = [*range(0, FAR, TILE), *range(FAR, width(items[index][1]) + 1, TILE)]
        return [(index, start, stop) for start, stop in zip(cuts[:-1], cuts[1:])]

    def score(index, start, stop):
        head, tile = items[index]
        rows = q_ref[tile * TILE : (tile + 1) * TILE, head * HD : (head + 1) * HD]
        found = jnp.dot(rows, kt[:, start:stop], preferred_element_type=jnp.float32)
        if stop <= FAR:
            found = found.reshape(TILE // SUBLANES, SUBLANES, TILE) + mask[:, start:stop][None]
            found = found.reshape(TILE, TILE)
        if stop == width(tile):
            found = jnp.where(causal, found, NEG)
        scores[index % 2][:, start:stop] = found
        peak = found[:, :HD]
        for at in range(HD, stop - start, HD):
            peak = jnp.maximum(peak, found[:, at : at + HD])
        peaks = (m0, m1)[index % 2]
        peaks[...] = peak if start == 0 else jnp.maximum(peaks[...], peak)

    for piece in pieces(0):
        score(*piece)
    for index, (head, tile) in enumerate(items):
        coming = pieces(index + 1) if index + 1 < len(items) else []
        total = width(tile)
        source, target, peaks = scores[index % 2], weights[index % 2], (m0, m1)[index % 2]
        largest = jnp.max(peaks[...], axis=1, keepdims=True)
        peaks[...] = jnp.broadcast_to(largest, (TILE, HD))
        for step in range(TILE // STEP):
            if step < len(coming):
                score(*coming[step])
            r0 = step * STEP
            most = jnp.concatenate([peaks[r0 : r0 + STEP, :]] * (total // HD), 1)
            target[r0 : r0 + STEP, :total] = jnp.exp2(
                (source[r0 : r0 + STEP, :total] - most) * SCALE
            ).astype(jnp.bfloat16)
        mixed = jnp.dot(target[:, :total], vx[:total, :], preferred_element_type=jnp.float32)
        at = (slice(tile * TILE, (tile + 1) * TILE), slice(head * HD, (head + 1) * HD))
        out_ref[at] = mixed[:, :HD] / mixed[:, HD:]
        log_ref[at] = peaks[...] * SCALE + jnp.log2(mixed[:, HD:])


def attention(queries, mine, other, keys, values):
    heads = queries.shape[1] // HD
    return pl.pallas_call(
        functools.partial(attention_kernel, heads),
        out_shape=[jax.ShapeDtypeStruct((ROWS, heads * HD), jnp.float32)] * 2,
        scratch_shapes=[
            pltpu.VMEM((FAR + ROWS, HD), jnp.bfloat16),
            pltpu.VMEM((HD, FAR + ROWS), jnp.bfloat16),
            pltpu.VMEM((SUBLANES, FAR), jnp.float32),
            pltpu.VMEM((FAR + ROWS, 2 * HD), jnp.bfloat16),
            pltpu.VMEM((TILE, FAR + ROWS), jnp.float32),
            pltpu.VMEM((TILE, FAR + ROWS), jnp.float32),
            pltpu.VMEM((TILE, FAR + ROWS), jnp.bfloat16),
            pltpu.VMEM((TILE, FAR + ROWS), jnp.bfloat16),
            pltpu.VMEM((TILE, HD), jnp.float32),
            pltpu.VMEM((TILE, HD), jnp.float32),
        ],
        compiler_params=pltpu.CompilerParams(vmem_limit_bytes=40 * 1024 * 1024),
    )(queries, mine, other, keys, values)


def join_kernel(heads, q_ref, part_ref, log_ref, *refs):
    *anchor_refs, out_ref = refs
    anchor = functools.reduce(jnp.add, [ref[...] for ref in anchor_refs])
    seen = lax.axis_index("ctx") > 0
    keys = anchor[:ANCHOR]
    values = jnp.concatenate([anchor[ANCHOR:], jnp.ones((ANCHOR, HD), jnp.bfloat16)], 1)
    for head in range(heads):
        columns = slice(head * HD, (head + 1) * HD)
        scores = lax.dot_general(
            q_ref[:, columns], keys, (((1,), (1,)), ((), ())), preferred_element_type=jnp.float32
        )
        scores = jnp.where(seen, scores, NEG)
        largest = jnp.max(scores, axis=1, keepdims=True)
        weights = jnp.exp2((scores - largest) * SCALE).astype(jnp.bfloat16)
        mixed = jnp.dot(weights, values, preferred_element_type=jnp.float32)
        before = log_ref[:, columns]
        top = jnp.maximum(before, largest * SCALE)
        old, new = jnp.exp2(before - top), jnp.exp2(largest * SCALE - top)
        out_ref[:, columns] = (
            (part_ref[:, columns] * old + mixed[:, :HD] * new) / (old + mixed[:, HD:] * new)
        ).astype(jnp.bfloat16)


def join(queries, part, log, anchors):
    return pl.pallas_call(
        functools.partial(join_kernel, queries.shape[1] // HD),
        out_shape=jax.ShapeDtypeStruct(queries.shape, jnp.bfloat16),
        compiler_params=pltpu.CompilerParams(vmem_limit_bytes=40 * 1024 * 1024),
    )(queries, part, log, *anchors)


def body(queries, keys, values, kept):
    sent, anchor = pick(kept, keys, values)
    up = lax.ppermute(anchor, "ctx", PAIRS_UP)
    sent, up = lax.optimization_barrier((sent, up))
    mine = lax.all_to_all(sent, "ctx", 0, 0, axis_index_groups=GROUPS_XY)
    anchor = anchor + up
    anchor = sum([lax.ppermute(anchor, "ctx", pairs) for pairs in PAIRS_X], anchor)
    for step in (4, 2):
        anchor = anchor + lax.ppermute(anchor, "ctx", PAIRS_Y[step])
    mine, anchor = lax.optimization_barrier((mine, anchor))
    anchors = [anchor, lax.ppermute(anchor, "ctx", PAIRS_Y[1])]
    other = lax.ppermute(mine, "ctx", PAIRS_CORE)

    part, log = attention(queries, mine, other, keys, values)
    attended = join(queries, part, log, anchors)
    return lax.all_to_all(attended, "head", split_axis=0, concat_axis=1, tiled=True)


def solution(mesh):
    return jax.shard_map(
        body,
        mesh=mesh,
        in_specs=(P("ctx", "head"), P("ctx", "head"), P("ctx", "head"), P("ctx", None)),
        out_specs=P(("ctx", "head"), None),
        check_vma=False,
    )
```

time: 81.1 us -> 78.4 us (0.967)
  the two profiles are of different devices: /device:TPU:43 before, /device:TPU:54 now
where the time goes in v2:
time: 78.4 us; the launch traced here: 78 us
  blocking collectives  30 us (38%)
  starting transfers between devices  18.4 us (23%)
  waiting for transfers between devices  16.3 us (21%)
  Pallas kernels  11.2 us (14%)
  other arithmetic  0.92 us (1%)
  local copies, waits for them, and re-layouts  0.91 us (1%)
    all_to_all x1, blocking collectives, body(): lax.all_to_all(attended, 'head', split_axis=0, concat_axis=1, tiled=True)  30 us
    ppermute x2, waiting for transfers between devices, body(): anchor = anchor + lax.ppermute(anchor, 'ctx', PAIRS_Y[step])  15.7 us
    all_to_all x1, starting transfers between devices, body(): mine = lax.all_to_all(sent, 'ctx', 0, 0, axis_index_groups=GROUPS_XY)  10.6 us
    pallas_call x1, Pallas kernels, attention(): pl.pallas_call(functools.partial(attention_kernel, heads), out_shape=[jax...  7.68 us
    pallas_call x1, Pallas kernels, pick(): pl.pallas_call(pick_kernel, out_shape=[jax.ShapeDtypeStruct((CHIPS, 2 * P...  2.12 us
    ppermute x3, starting transfers between devices, body(): lax.ppermute(anchor, 'ctx', pairs)  1.99 us
    ppermute x2, starting transfers between devices, body(): anchor = anchor + lax.ppermute(anchor, 'ctx', PAIRS_Y[step])  1.96 us
    ppermute x1, starting transfers between devices, body(): other = lax.ppermute(mine, 'ctx', PAIRS_CORE)  1.92 us
  transfers between devices with their start and end apart: 9, of which 2 were waited for; matrix products, arithmetic and copies ran while one was open for 1% of the time, Pallas kernels for 10%

profile of v2, /device:TPU:54, one launch (start us, length us, event | category | flops | bytes accessed | tf_op | source)
XLA Modules:
  0.0 78.0 jit_solution(9945813074911543298)
XLA Ops:
  0.0 0.0 copy-start.1
  0.0 0.0 copy-start.2
  0.0 0.0 copy-start
  0.0 2.1 %shard_map.46 = (bf16[32,64,128]{2,1,0:T(8,128)(2,1)}, bf16[256,128]{1,0:T(8,128)(2,1)}) custom-call(s32[1,32]{1,0:T(1,128)} %kept_ref.1, bf16[512,128]{1,0:T(8,128)(2,1)} %key_ref.3, bf16[512,128]{1,0:T(8,128)(2,1)} %value_ref.3), custom_call_target="tpu_custom_call" | custom-call | tf_op jit(solution)/shard_map/pallas_call | solution.py:61
  2.1 0.7 collective-permute-start
  2.8 0.0 collective-permute-done
  2.8 10.6 %all-to-all-start = ((bf16[32,64,128]{2,1,0:T(8,128)(2,1)}), bf16[32,64,128]{2,1,0:T(8,128)(2,1)S(1)}, u32[]{:S(2)}, u32[]{:S(2)}) async-start(bf16[32,64,128]{2,1,0:T(8,128)(2,1)} %get-tuple-element.15), calls=%async_computation | async-start | bytes 1048576 | tf_op jit(solution)/shard_map/all_to_all | solution.py:201
  13.4 0.9 %add.18 = bf16[256,128]{1,0:T(8,128)(2,1)S(1)} add(bf16[256,128]{1,0:T(8,128)(2,1)} %get-tuple-element.14, bf16[256,128]{1,0:T(8,128)(2,1)S(1)} %collective-permute-done) | non-fusion elementwise | flops 32768 | bytes 196608 | tf_op jit(solution)/shard_map/add | solution.py:202
  14.3 0.7 collective-permute-start.1
  15.0 0.7 collective-permute-start.2
  15.6 0.7 collective-permute-start.3
  16.3 0.0 collective-permute-done.1
  16.3 0.0 collective-permute-done.2
  16.3 0.0 collective-permute-done.3
  16.4 0.7 collective-permute-start.4
  17.0 0.0 collective-permute-done.4
  17.1 1.3 %collective-permute-start.5 = (bf16[256,128]{1,0:T(8,128)(2,1)S(1)}, bf16[256,128]{1,0:T(8,128)(2,1)S(1)}, u32[]{:S(2)}, u32[]{:S(2)}) collective-permute-start(bf16[256,128]{1,0:T(8,128)(2,1)S(1)} %add.22), channel_id=1, source_target_pairs={{0,32},{8,40},{64,96},{72,104},{128,160},{136,168},{192,224},{200,... | collective-permute-start | bytes 196616 | tf_op jit(solution)/shard_map/ppermute | solution.py:205
  18.4 15.7 %collective-permute-done.5 = bf16[256,128]{1,0:T(8,128)(2,1)S(1)} collective-permute-done((bf16[256,128]{1,0:T(8,128)(2,1)S(1)}, bf16[256,128]{1,0:T(8,128)(2,1)S(1)}, u32[]{:S(2)}, u32[]{:S(2)}) %collective-permute-start.5) | collective-permute-done | bytes 65568 | tf_op jit(solution)/shard_map/ppermute | solution.py:205
  34.1 0.0 all-to-all-done.mine_ref
  34.1 1.9 %collective-permute-start.6 = (bf16[32,64,128]{2,1,0:T(8,128)(2,1)S(1)}, bf16[32,64,128]{2,1,0:T(8,128)(2,1)S(1)}, u32[]{:S(2)}, u32[]{:S(2)}) collective-permute-start(bf16[32,64,128]{2,1,0:T(8,128)(2,1)S(1)} %all-to-all-done.mine_ref), channel_id=1, source_target_pairs={{0,8},{8,0},{16,24},{24,16},{32,40},{40,32},{48,56},{56,48},{64,72... | collective-permute-start | bytes 1572872 | tf_op jit(solution)/shard_map/ppermute | solution.py:208
  36.1 1.3 %collective-permute-start.7 = (bf16[256,128]{1,0:T(8,128)(2,1)S(1)}, bf16[256,128]{1,0:T(8,128)(2,1)S(1)}, u32[]{:S(2)}, u32[]{:S(2)}) collective-permute-start(bf16[256,128]{1,0:T(8,128)(2,1)S(1)} %add.23.refs_0_), channel_id=1, source_target_pairs={{0,16},{8,24},{32,48},{40,56},{64,80},{72,88},{96,112},{104,120},{... | collective-permute-start | bytes 196616 | tf_op jit(solution)/shard_map/ppermute | solution.py:207
  37.4 0.6 collective-permute-done.6.other_ref
  38.0 0.0 copy-done.1
  38.0 0.0 copy-done.2
  38.0 0.0 copy-done
  38.0 7.7 %shard_map.47 = (f32[512,640]{1,0:T(8,128)S(1)}, f32[512,640]{1,0:T(8,128)S(1)}) custom-call(bf16[512,640]{1,0:T(8,128)(2,1)S(1)} %copy-done, bf16[32,64,128]{2,1,0:T(8,128)(2,1)S(1)} %all-to-all-done.mine_ref, bf16[32,64,128]{2,1,0:T(8,128)(2,1)S(1)} %collective-permute-done.6.other_ref, bf16[512,128]{1,0:T(8,128)(2,1)S(1)} %copy-done.1, ...), custom_call_target="tpu_custom_call" | custom-call | tf_op jit(solution)/shard_map/pallas_call | solution.py:147
  45.7 0.0 collective-permute-done.7.refs_1_
  45.7 1.4 %shard_map.48 = bf16[512,640]{1,0:T(8,128)(2,1)S(1)} custom-call(bf16[512,640]{1,0:T(8,128)(2,1)S(1)} %copy-done, f32[512,640]{1,0:T(8,128)S(1)} %get-tuple-element.18.part_ref, f32[512,640]{1,0:T(8,128)S(1)} %get-tuple-element.19.log_ref, bf16[256,128]{1,0:T(8,128)(2,1)S(1)} %add.23.refs_0_, bf16[256,128]{1,0:T(8,128)(2,1)S(1)} %collective-permute-done.7.refs_1_), custom_call_target="tpu_custom_call" | custom-call | tf_op jit(solution)/shard_map/pallas_call | solution.py:190
  47.1 30.0 %all_to_all.24 = bf16[8,64,640]{2,1,0:T(8,128)(2,1)S(1)} all-to-all(bf16[8,64,640]{2,1,0:T(8,128)(2,1)S(1)} %bitcast.4), channel_id=1, replica_groups=mesh['ctx'=64,'head'=8] {'head'}, dimensions={0} | all-to-all | bytes 1310720 | tf_op jit(solution)/shard_map/all_to_all | solution.py:212
  77.1 0.9 %copy.6 = bf16[8,8,8,640]{3,2,0,1:T(8,128)(2,1)} copy(bf16[8,8,8,640]{3,2,1,0:T(8,128)(2,1)S(1)} %bitcast.5) | data formatting | bytes 1310720 | tf_op jit(solution)/shard_map/all_to_all | solution.py:212
  (3 shorter events, 0.1 us)
Async XLA Ops:
  0.0 38.0 %copy-start.1 = (bf16[512,128]{1,0:T(8,128)(2,1)S(1)}, bf16[512,128]{1,0:T(8,128)(2,1)}, u32[]{:S(2)}) copy-start(bf16[512,128]{1,0:T(8,128)(2,1)} %key_ref.3) | copy-start | bytes 393220
  0.0 38.0 %copy-start.2 = (bf16[512,128]{1,0:T(8,128)(2,1)S(1)}, bf16[512,128]{1,0:T(8,128)(2,1)}, u32[]{:S(2)}) copy-start(bf16[512,128]{1,0:T(8,128)(2,1)} %value_ref.3) | copy-start | bytes 393220
  0.0 38.0 %copy-start = (bf16[512,640]{1,0:T(8,128)(2,1)S(1)}, bf16[512,640]{1,0:T(8,128)(2,1)}, u32[]{:S(2)}) copy-start(bf16[512,640]{1,0:T(8,128)(2,1)} %q_ref.3) | copy-start | bytes 1966084
  2.1 0.7 collective-permute-start
  2.8 31.3 %all-to-all-start = ((bf16[32,64,128]{2,1,0:T(8,128)(2,1)}), bf16[32,64,128]{2,1,0:T(8,128)(2,1)S(1)}, u32[]{:S(2)}, u32[]{:S(2)}) async-start(bf16[32,64,128]{2,1,0:T(8,128)(2,1)} %get-tuple-element.15), calls=%async_computation | async-start | bytes 1048576 | tf_op jit(solution)/shard_map/all_to_all | solution.py:201
  14.3 2.0 %collective-permute-start.1 = (bf16[256,128]{1,0:T(8,128)(2,1)S(1)}, bf16[256,128]{1,0:T(8,128)(2,1)S(1)}, u32[]{:S(2)}, u32[]{:S(2)}) collective-permute-start(bf16[256,128]{1,0:T(8,128)(2,1)S(1)} %add.18), channel_id=1, source_target_pairs={{0,128},{8,136},{1,129},{9,137},{2,130},{10,138},{3,131},{11,139},... | collective-permute-start | bytes 196616 | tf_op jit(solution)/shard_map/ppermute | solution.py:203
  15.0 1.4 %collective-permute-start.2 = (bf16[256,128]{1,0:T(8,128)(2,1)S(1)}, bf16[256,128]{1,0:T(8,128)(2,1)S(1)}, u32[]{:S(2)}, u32[]{:S(2)}) collective-permute-start(bf16[256,128]{1,0:T(8,128)(2,1)S(1)} %add.18), channel_id=1, source_target_pairs={{0,256},{8,264},{1,257},{9,265},{2,258},{10,266},{3,259},{11,267},... | collective-permute-start | bytes 196616 | tf_op jit(solution)/shard_map/ppermute | solution.py:203
  15.6 0.7 collective-permute-start.3
  16.4 0.7 collective-permute-start.4
  17.1 17.0 %collective-permute-start.5 = (bf16[256,128]{1,0:T(8,128)(2,1)S(1)}, bf16[256,128]{1,0:T(8,128)(2,1)S(1)}, u32[]{:S(2)}, u32[]{:S(2)}) collective-permute-start(bf16[256,128]{1,0:T(8,128)(2,1)S(1)} %add.22), channel_id=1, source_target_pairs={{0,32},{8,40},{64,96},{72,104},{128,160},{136,168},{192,224},{200,... | collective-permute-start | bytes 196616 | tf_op jit(solution)/shard_map/ppermute | solution.py:205
  34.1 3.8 %collective-permute-start.6 = (bf16[32,64,128]{2,1,0:T(8,128)(2,1)S(1)}, bf16[32,64,128]{2,1,0:T(8,128)(2,1)S(1)}, u32[]{:S(2)}, u32[]{:S(2)}) collective-permute-start(bf16[32,64,128]{2,1,0:T(8,128)(2,1)S(1)} %all-to-all-done.mine_ref), channel_id=1, source_target_pairs={{0,8},{8,0},{16,24},{24,16},{32,40},{40,32},{48,56},{56,48},{64,72... | collective-permute-start | bytes 1572872 | tf_op jit(solution)/shard_map/ppermute | solution.py:208
  36.1 9.6 %collective-permute-start.7 = (bf16[256,128]{1,0:T(8,128)(2,1)S(1)}, bf16[256,128]{1,0:T(8,128)(2,1)S(1)}, u32[]{:S(2)}, u32[]{:S(2)}) collective-permute-start(bf16[256,128]{1,0:T(8,128)(2,1)S(1)} %add.23.refs_0_), channel_id=1, source_target_pairs={{0,16},{8,24},{32,48},{40,56},{64,80},{72,88},{96,112},{104,120},{... | collective-permute-start | bytes 196616 | tf_op jit(solution)/shard_map/ppermute | solution.py:207

commit v3 on v2

--- a/solution.py
+++ b/solution.py
@@ -18,7 +18,6 @@
 ROWS = 512
 TILE = 256
 STEP = 16
-SUBLANES = 8
 NEG = -1e30
 SCALE = math.log2(math.e) / math.sqrt(HD)
 
@@ -30,15 +29,10 @@
 GROUPS_XY = [[ctx_of(x, y, c) for x in range(NX) for y in range(NY)] for c in range(NC)]
 PAIRS_UP = [(0, 1)]
 PAIRS_X = [[(c, ctx_of(x, 0, c)) for c in range(NC)] for x in range(1, NX)]
-PAIRS_Y = {
-    step: [
-        (ctx_of(x, y, c), ctx_of(x, y + step, c))
-        for x in range(NX)
-        for y in range(0, NY, 2 * step)
-        for c in range(NC)
-    ]
-    for step in (4, 2, 1)
-}
+PAIRS_Y = [
+    [(ctx_of(x, y, c), ctx_of(x, to, c)) for x in range(NX) for y, to in hops for c in range(NC)]
+    for hops in ([(0, 6)], [(0, 2), (6, 4)], [(0, 1), (2, 3), (4, 5), (6, 7)])
+]
 PAIRS_CORE = [(i, i ^ 1) for i in range(NX * NY * NC)]
 
 
@@ -69,7 +63,7 @@
 
 def attention_kernel(
     heads, q_ref, mine_ref, other_ref, key_ref, value_ref, out_ref, log_ref,
-    kx, kt, mask, vx, s0, s1, p0, p1, m0, m1,
+    kx, kt, vx, s0, s1, p0, p1, m0, m1,
 ):
     me = lax.axis_index("ctx")
     core = lax.rem(me, NC)
@@ -84,12 +78,17 @@
     vx[:, HD:] = jnp.ones((FAR + ROWS, HD), jnp.bfloat16)
 
     for start in range(0, FAR + ROWS, HD):
-        kt[:, start : start + HD] = kx[start : start + HD, :].T
-    at = lax.broadcasted_iota(jnp.int32, (SUBLANES, HALF), 1)
+        kt[:HD, start : start + HD] = kx[start : start + HD, :].T
+    row = lax.broadcasted_iota(jnp.int32, (HD, HALF), 0)
+    at = lax.broadcasted_iota(jnp.int32, (HD, HALF), 1)
+    never = jnp.where(row == 0, NEG, 0.0)
     for owner_core, base in ((core, 0), (1 - core, HALF)):
         owner = NC * (at >> 5) + owner_core
-        mask[:, base : base + HALF] = jnp.where(owner < me, 0.0, NEG)
-
+        kt[HD:, base : base + HALF] = jnp.where(owner < me, 0.0, never).astype(jnp.bfloat16)
+    kt[HD:, FAR:] = jnp.zeros((HD, ROWS), jnp.bfloat16)
+
+    lane = lax.broadcasted_iota(jnp.int32, (TILE, HD), 1)
+    flag = jnp.where(lane == 0, 1.0, 0.0).astype(jnp.bfloat16)
     items = [(head, tile) for head in range(heads) for tile in range(ROWS // TILE)]
     scores, weights = (s0, s1), (p0, p1)
 
@@ -107,10 +106,8 @@
     def score(index, start, stop):
         head, tile = items[index]
         rows = q_ref[tile * TILE : (tile + 1) * TILE, head * HD : (head + 1) * HD]
-        found = jnp.dot(rows, kt[:, start:stop], preferred_element_type=jnp.float32)
-        if stop <= FAR:
-            found = found.reshape(TILE // SUBLANES, SUBLANES, TILE) + mask[:, start:stop][None]
-            found = found.reshape(TILE, TILE)
+        queries = jnp.concatenate([rows, flag], 1)
+        found = jnp.dot(queries, kt[:, start:stop], preferred_element_type=jnp.float32)
         if stop == width(tile):
             found = jnp.where(causal, found, NEG)
         scores[index % 2][:, start:stop] = found
@@ -149,8 +146,7 @@
         out_shape=[jax.ShapeDtypeStruct((ROWS, heads * HD), jnp.float32)] * 2,
         scratch_shapes=[
             pltpu.VMEM((FAR + ROWS, HD), jnp.bfloat16),
-            pltpu.VMEM((HD, FAR + ROWS), jnp.bfloat16),
-            pltpu.VMEM((SUBLANES, FAR), jnp.float32),
+            pltpu.VMEM((2 * HD, FAR + ROWS), jnp.bfloat16),
             pltpu.VMEM((FAR + ROWS, 2 * HD), jnp.bfloat16),
             pltpu.VMEM((TILE, FAR + ROWS), jnp.float32),
             pltpu.VMEM((TILE, FAR + ROWS), jnp.float32),
@@ -201,10 +197,10 @@
     mine = lax.all_to_all(sent, "ctx", 0, 0, axis_index_groups=GROUPS_XY)
     anchor = anchor + up
     anchor = sum([lax.ppermute(anchor, "ctx", pairs) for pairs in PAIRS_X], anchor)
-    for step in (4, 2):
-        anchor = anchor + lax.ppermute(anchor, "ctx", PAIRS_Y[step])
+    for pairs in PAIRS_Y[:2]:
+        anchor = anchor + lax.ppermute(anchor, "ctx", pairs)
     mine, anchor = lax.optimization_barrier((mine, anchor))
-    anchors = [anchor, lax.ppermute(anchor, "ctx", PAIRS_Y[1])]
+    anchors = [anchor, lax.ppermute(anchor, "ctx", PAIRS_Y[2])]
     other = lax.ppermute(mine, "ctx", PAIRS_CORE)
 
     part, log = attention(queries, mine, other, keys, values)

time: 78.4 us -> 77.1 us (0.983)
  the two profiles are of different devices: /device:TPU:54 before, /device:TPU:6 now
where the time goes in v3:
time: 77.1 us; the launch traced here: 75.6 us
  blocking collectives  29.1 us (38%)
  starting transfers between devices  22.8 us (30%)
  Pallas kernels  11 us (14%)
  waiting for transfers between devices  10.8 us (14%)
  other arithmetic  0.92 us (1%)
  local copies, waits for them, and re-layouts  0.91 us (1%)
    all_to_all x1, blocking collectives, body(): lax.all_to_all(attended, 'head', split_axis=0, concat_axis=1, tiled=True)  29.1 us
    all_to_all x1, starting transfers between devices, body(): mine = lax.all_to_all(sent, 'ctx', 0, 0, axis_index_groups=GROUPS_XY)  11.3 us
    pallas_call x1, Pallas kernels, attention(): pl.pallas_call(functools.partial(attention_kernel, heads), out_shape=[jax...  7.5 us
    ppermute x3, waiting for transfers between devices, body(): lax.ppermute(anchor, 'ctx', pairs)  6.98 us
    ppermute x2, waiting for transfers between devices, body(): anchor = anchor + lax.ppermute(anchor, 'ctx', pairs)  3.77 us
    ppermute x1, starting transfers between devices, body(): anchors = [anchor, lax.ppermute(anchor, 'ctx', PAIRS_Y[2])]  3.71 us
    ppermute x3, starting transfers between devices, body(): lax.ppermute(anchor, 'ctx', pairs)  2.62 us
    ppermute x2, starting transfers between devices, body(): anchor = anchor + lax.ppermute(anchor, 'ctx', pairs)  2.59 us
  transfers between devices with their start and end apart: 9, of which 3 were waited for; matrix products, arithmetic and copies ran while one was open for 1% of the time, Pallas kernels for 10%

profile of v3, /device:TPU:6, one launch (start us, length us, event | category | flops | bytes accessed | tf_op | source)
XLA Modules:
  0.0 75.6 jit_solution(15923650705625369697)
XLA Ops:
  0.0 0.0 copy-start.1
  0.0 0.0 copy-start.2
  0.0 0.0 copy-start
  0.0 2.1 %shard_map.46 = (bf16[32,64,128]{2,1,0:T(8,128)(2,1)}, bf16[256,128]{1,0:T(8,128)(2,1)}) custom-call(s32[1,32]{1,0:T(1,128)} %kept_ref.1, bf16[512,128]{1,0:T(8,128)(2,1)} %key_ref.3, bf16[512,128]{1,0:T(8,128)(2,1)} %value_ref.3), custom_call_target="tpu_custom_call" | custom-call | tf_op jit(solution)/shard_map/pallas_call | solution.py:55
  2.1 0.7 collective-permute-start
  2.8 0.0 collective-permute-done
  2.8 11.3 %all-to-all-start = ((bf16[32,64,128]{2,1,0:T(8,128)(2,1)}), bf16[32,64,128]{2,1,0:T(8,128)(2,1)S(1)}, u32[]{:S(2)}, u32[]{:S(2)}) async-start(bf16[32,64,128]{2,1,0:T(8,128)(2,1)} %get-tuple-element.15), calls=%async_computation | async-start | bytes 1048576 | tf_op jit(solution)/shard_map/all_to_all | solution.py:197
  14.1 0.9 %add.18 = bf16[256,128]{1,0:T(8,128)(2,1)S(1)} add(bf16[256,128]{1,0:T(8,128)(2,1)} %get-tuple-element.14, bf16[256,128]{1,0:T(8,128)(2,1)S(1)} %collective-permute-done) | non-fusion elementwise | flops 32768 | bytes 196608 | tf_op jit(solution)/shard_map/add | solution.py:198
  14.9 0.7 collective-permute-start.1
  15.6 0.7 collective-permute-start.2
  16.3 1.3 %collective-permute-start.3 = (bf16[256,128]{1,0:T(8,128)(2,1)S(1)}, bf16[256,128]{1,0:T(8,128)(2,1)S(1)}, u32[]{:S(2)}, u32[]{:S(2)}) collective-permute-start(bf16[256,128]{1,0:T(8,128)(2,1)S(1)} %add.18), channel_id=1, source_target_pairs={{0,384},{8,392},{1,385},{9,393},{2,386},{10,394},{3,387},{11,395},... | collective-permute-start | bytes 196616 | tf_op jit(solution)/shard_map/ppermute | solution.py:199
  17.6 0.0 collective-permute-done.1
  17.6 0.0 collective-permute-done.2
  17.6 7.0 %collective-permute-done.3 = bf16[256,128]{1,0:T(8,128)(2,1)S(1)} collective-permute-done((bf16[256,128]{1,0:T(8,128)(2,1)S(1)}, bf16[256,128]{1,0:T(8,128)(2,1)S(1)}, u32[]{:S(2)}, u32[]{:S(2)}) %collective-permute-start.3) | collective-permute-done | bytes 65568 | tf_op jit(solution)/shard_map/ppermute | solution.py:199
  24.6 1.3 %collective-permute-start.4 = (bf16[256,128]{1,0:T(8,128)(2,1)S(1)}, bf16[256,128]{1,0:T(8,128)(2,1)S(1)}, u32[]{:S(2)}, u32[]{:S(2)}) collective-permute-start(bf16[256,128]{1,0:T(8,128)(2,1)S(1)} %add_add_fusion), channel_id=1, source_target_pairs={{0,96},{8,104},{128,224},{136,232},{256,352},{264,360},{384,480},{... | collective-permute-start | bytes 196616 | tf_op jit(solution)/shard_map/ppermute | solution.py:201
  25.9 1.9 %collective-permute-done.4 = bf16[256,128]{1,0:T(8,128)(2,1)S(1)} collective-permute-done((bf16[256,128]{1,0:T(8,128)(2,1)S(1)}, bf16[256,128]{1,0:T(8,128)(2,1)S(1)}, u32[]{:S(2)}, u32[]{:S(2)}) %collective-permute-start.4) | collective-permute-done | bytes 65568 | tf_op jit(solution)/shard_map/ppermute | solution.py:201
  27.8 1.3 %collective-permute-start.5 = (bf16[256,128]{1,0:T(8,128)(2,1)S(1)}, bf16[256,128]{1,0:T(8,128)(2,1)S(1)}, u32[]{:S(2)}, u32[]{:S(2)}) collective-permute-start(bf16[256,128]{1,0:T(8,128)(2,1)S(1)} %add.22), channel_id=1, source_target_pairs={{0,32},{8,40},{96,64},{104,72},{128,160},{136,168},{224,192},{232,... | collective-permute-start | bytes 196616 | tf_op jit(solution)/shard_map/ppermute | solution.py:201
  29.1 1.9 %collective-permute-done.5 = bf16[256,128]{1,0:T(8,128)(2,1)S(1)} collective-permute-done((bf16[256,128]{1,0:T(8,128)(2,1)S(1)}, bf16[256,128]{1,0:T(8,128)(2,1)S(1)}, u32[]{:S(2)}, u32[]{:S(2)}) %collective-permute-start.5) | collective-permute-done | bytes 65568 | tf_op jit(solution)/shard_map/ppermute | solution.py:201
  31.0 0.0 all-to-all-done.mine_ref
  31.0 1.9 %collective-permute-start.6 = (bf16[32,64,128]{2,1,0:T(8,128)(2,1)S(1)}, bf16[32,64,128]{2,1,0:T(8,128)(2,1)S(1)}, u32[]{:S(2)}, u32[]{:S(2)}) collective-permute-start(bf16[32,64,128]{2,1,0:T(8,128)(2,1)S(1)} %all-to-all-done.mine_ref), channel_id=1, source_target_pairs={{0,8},{8,0},{16,24},{24,16},{32,40},{40,32},{48,56},{56,48},{64,72... | collective-permute-start | bytes 1572872 | tf_op jit(solution)/shard_map/ppermute | solution.py:204
  32.9 3.7 %collective-permute-start.7 = (bf16[256,128]{1,0:T(8,128)(2,1)S(1)}, bf16[256,128]{1,0:T(8,128)(2,1)S(1)}, u32[]{:S(2)}, u32[]{:S(2)}) collective-permute-start(bf16[256,128]{1,0:T(8,128)(2,1)S(1)} %add.23.refs_0_), channel_id=1, source_target_pairs={{0,16},{8,24},{32,48},{40,56},{64,80},{72,88},{96,112},{104,120},{... | collective-permute-start | bytes 196616 | tf_op jit(solution)/shard_map/ppermute | solution.py:203
  36.7 0.0 collective-permute-done.6.other_ref
  36.7 0.0 copy-done.1
  36.7 0.0 copy-done.2
  36.7 0.0 copy-done
  36.7 7.5 %shard_map.47 = (f32[512,640]{1,0:T(8,128)S(1)}, f32[512,640]{1,0:T(8,128)S(1)}) custom-call(bf16[512,640]{1,0:T(8,128)(2,1)S(1)} %copy-done, bf16[32,64,128]{2,1,0:T(8,128)(2,1)S(1)} %all-to-all-done.mine_ref, bf16[32,64,128]{2,1,0:T(8,128)(2,1)S(1)} %collective-permute-done.6.other_ref, bf16[512,128]{1,0:T(8,128)(2,1)S(1)} %copy-done.1, ...), custom_call_target="tpu_custom_call" | custom-call | tf_op jit(solution)/shard_map/pallas_call | solution.py:144
  44.2 0.0 collective-permute-done.7.refs_1_
  44.2 1.4 %shard_map.48 = bf16[512,640]{1,0:T(8,128)(2,1)S(1)} custom-call(bf16[512,640]{1,0:T(8,128)(2,1)S(1)} %copy-done, f32[512,640]{1,0:T(8,128)S(1)} %get-tuple-element.18.part_ref, f32[512,640]{1,0:T(8,128)S(1)} %get-tuple-element.19.log_ref, bf16[256,128]{1,0:T(8,128)(2,1)S(1)} %add.23.refs_0_, bf16[256,128]{1,0:T(8,128)(2,1)S(1)} %collective-permute-done.7.refs_1_), custom_call_target="tpu_custom_call" | custom-call | tf_op jit(solution)/shard_map/pallas_call | solution.py:186
  45.6 29.1 %all_to_all.24 = bf16[8,64,640]{2,1,0:T(8,128)(2,1)S(1)} all-to-all(bf16[8,64,640]{2,1,0:T(8,128)(2,1)S(1)} %bitcast.4), channel_id=1, replica_groups=mesh['ctx'=64,'head'=8] {'head'}, dimensions={0} | all-to-all | bytes 1310720 | tf_op jit(solution)/shard_map/all_to_all | solution.py:208
  74.7 0.9 %copy.6 = bf16[8,8,8,640]{3,2,0,1:T(8,128)(2,1)} copy(bf16[8,8,8,640]{3,2,1,0:T(8,128)(2,1)S(1)} %bitcast.5) | data formatting | bytes 1310720 | tf_op jit(solution)/shard_map/all_to_all | solution.py:208
  (3 shorter events, 0.1 us)
Async XLA Ops:
  0.0 36.7 %copy-start.1 = (bf16[512,128]{1,0:T(8,128)(2,1)S(1)}, bf16[512,128]{1,0:T(8,128)(2,1)}, u32[]{:S(2)}) copy-start(bf16[512,128]{1,0:T(8,128)(2,1)} %key_ref.3) | copy-start | bytes 393220
  0.0 36.7 %copy-start.2 = (bf16[512,128]{1,0:T(8,128)(2,1)S(1)}, bf16[512,128]{1,0:T(8,128)(2,1)}, u32[]{:S(2)}) copy-start(bf16[512,128]{1,0:T(8,128)(2,1)} %value_ref.3) | copy-start | bytes 393220
  0.0 36.7 %copy-start = (bf16[512,640]{1,0:T(8,128)(2,1)S(1)}, bf16[512,640]{1,0:T(8,128)(2,1)}, u32[]{:S(2)}) copy-start(bf16[512,640]{1,0:T(8,128)(2,1)} %q_ref.3) | copy-start | bytes 1966084
  2.1 0.7 collective-permute-start
  2.8 28.2 %all-to-all-start = ((bf16[32,64,128]{2,1,0:T(8,128)(2,1)}), bf16[32,64,128]{2,1,0:T(8,128)(2,1)S(1)}, u32[]{:S(2)}, u32[]{:S(2)}) async-start(bf16[32,64,128]{2,1,0:T(8,128)(2,1)} %get-tuple-element.15), calls=%async_computation | async-start | bytes 1048576 | tf_op jit(solution)/shard_map/all_to_all | solution.py:197
  14.9 2.6 %collective-permute-start.1 = (bf16[256,128]{1,0:T(8,128)(2,1)S(1)}, bf16[256,128]{1,0:T(8,128)(2,1)S(1)}, u32[]{:S(2)}, u32[]{:S(2)}) collective-permute-start(bf16[256,128]{1,0:T(8,128)(2,1)S(1)} %add.18), channel_id=1, source_target_pairs={{0,128},{8,136},{1,129},{9,137},{2,130},{10,138},{3,131},{11,139},... | collective-permute-start | bytes 196616 | tf_op jit(solution)/shard_map/ppermute | solution.py:199
  15.6 2.0 %collective-permute-start.2 = (bf16[256,128]{1,0:T(8,128)(2,1)S(1)}, bf16[256,128]{1,0:T(8,128)(2,1)S(1)}, u32[]{:S(2)}, u32[]{:S(2)}) collective-permute-start(bf16[256,128]{1,0:T(8,128)(2,1)S(1)} %add.18), channel_id=1, source_target_pairs={{0,256},{8,264},{1,257},{9,265},{2,258},{10,266},{3,259},{11,267},... | collective-permute-start | bytes 196616 | tf_op jit(solution)/shard_map/ppermute | solution.py:199
  16.3 8.3 %collective-permute-start.3 = (bf16[256,128]{1,0:T(8,128)(2,1)S(1)}, bf16[256,128]{1,0:T(8,128)(2,1)S(1)}, u32[]{:S(2)}, u32[]{:S(2)}) collective-permute-start(bf16[256,128]{1,0:T(8,128)(2,1)S(1)} %add.18), channel_id=1, source_target_pairs={{0,384},{8,392},{1,385},{9,393},{2,386},{10,394},{3,387},{11,395},... | collective-permute-start | bytes 196616 | tf_op jit(solution)/shard_map/ppermute | solution.py:199
  24.6 3.2 %collective-permute-start.4 = (bf16[256,128]{1,0:T(8,128)(2,1)S(1)}, bf16[256,128]{1,0:T(8,128)(2,1)S(1)}, u32[]{:S(2)}, u32[]{:S(2)}) collective-permute-start(bf16[256,128]{1,0:T(8,128)(2,1)S(1)} %add_add_fusion), channel_id=1, source_target_pairs={{0,96},{8,104},{128,224},{136,232},{256,352},{264,360},{384,480},{... | collective-permute-start | bytes 196616 | tf_op jit(solution)/shard_map/ppermute | solution.py:201
  27.8 3.2 %collective-permute-start.5 = (bf16[256,128]{1,0:T(8,128)(2,1)S(1)}, bf16[256,128]{1,0:T(8,128)(2,1)S(1)}, u32[]{:S(2)}, u32[]{:S(2)}) collective-permute-start(bf16[256,128]{1,0:T(8,128)(2,1)S(1)} %add.22), channel_id=1, source_target_pairs={{0,32},{8,40},{96,64},{104,72},{128,160},{136,168},{224,192},{232,... | collective-permute-start | bytes 196616 | tf_op jit(solution)/shard_map/ppermute | solution.py:201
  31.0 5.7 %collective-permute-start.6 = (bf16[32,64,128]{2,1,0:T(8,128)(2,1)S(1)}, bf16[32,64,128]{2,1,0:T(8,128)(2,1)S(1)}, u32[]{:S(2)}, u32[]{:S(2)}) collective-permute-start(bf16[32,64,128]{2,1,0:T(8,128)(2,1)S(1)} %all-to-all-done.mine_ref), channel_id=1, source_target_pairs={{0,8},{8,0},{16,24},{24,16},{32,40},{40,32},{48,56},{56,48},{64,72... | collective-permute-start | bytes 1572872 | tf_op jit(solution)/shard_map/ppermute | solution.py:204
  32.9 11.3 %collective-permute-start.7 = (bf16[256,128]{1,0:T(8,128)(2,1)S(1)}, bf16[256,128]{1,0:T(8,128)(2,1)S(1)}, u32[]{:S(2)}, u32[]{:S(2)}) collective-permute-start(bf16[256,128]{1,0:T(8,128)(2,1)S(1)} %add.23.refs_0_), channel_id=1, source_target_pairs={{0,16},{8,24},{32,48},{40,56},{64,80},{72,88},{96,112},{104,120},{... | collective-permute-start | bytes 196616 | tf_op jit(solution)/shard_map/ppermute | solution.py:203

commit v4 on v3

--- a/solution.py
+++ b/solution.py
@@ -16,8 +16,10 @@
 HALF = CHIPS * PASS
 FAR = 2 * HALF
 ROWS = 512
-TILE = 256
+TILE = 512
+SPAN = 256
 STEP = 16
+PACE = 3
 NEG = -1e30
 SCALE = math.log2(math.e) / math.sqrt(HD)
 
@@ -92,15 +94,15 @@
     items = [(head, tile) for head in range(heads) for tile in range(ROWS // TILE)]
     scores, weights = (s0, s1), (p0, p1)
 
-    causal = lax.broadcasted_iota(jnp.int32, (TILE, TILE), 1) <= lax.broadcasted_iota(
-        jnp.int32, (TILE, TILE), 0
+    ahead = lax.broadcasted_iota(jnp.int32, (TILE, SPAN), 1) - lax.broadcasted_iota(
+        jnp.int32, (TILE, SPAN), 0
     )
 
     def width(tile):
         return FAR + (tile + 1) * TILE
 
     def pieces(index):
-        cuts = [*range(0, FAR, TILE), *range(FAR, width(items[index][1]) + 1, TILE)]
+        cuts = range(0, width(items[index][1]) + 1, SPAN)
         return [(index, start, stop) for start, stop in zip(cuts[:-1], cuts[1:])]
 
     def score(index, start, stop):
@@ -108,8 +110,8 @@
         rows = q_ref[tile * TILE : (tile + 1) * TILE, head * HD : (head + 1) * HD]
         queries = jnp.concatenate([rows, flag], 1)
         found = jnp.dot(queries, kt[:, start:stop], preferred_element_type=jnp.float32)
-        if stop == width(tile):
-            found = jnp.where(causal, found, NEG)
+        if stop > FAR + tile * TILE:
+            found = jnp.where(ahead <= FAR + tile * TILE - start, found, NEG)
         scores[index % 2][:, start:stop] = found
         peak = found[:, :HD]
         for at in range(HD, stop - start, HD):
@@ -126,8 +128,8 @@
         largest = jnp.max(peaks[...], axis=1, keepdims=True)
         peaks[...] = jnp.broadcast_to(largest, (TILE, HD))
         for step in range(TILE // STEP):
-            if step < len(coming):
-                score(*coming[step])
+            if step % PACE == 0 and step // PACE < len(coming):
+                score(*coming[step // PACE])
             r0 = step * STEP
             most = jnp.concatenate([peaks[r0 : r0 + STEP, :]] * (total // HD), 1)
             target[r0 : r0 + STEP, :total] = jnp.exp2(

time: 77.1 us -> 77.5 us (level)
  no operation moved by 1% of the time
where the time goes in v4:
time: 77.5 us; the launch traced here: 76 us
  blocking collectives  29.1 us (38%)
  starting transfers between devices  22.8 us (29%)
  Pallas kernels  11.4 us (15%)
  waiting for transfers between devices  10.8 us (14%)
  other arithmetic  0.92 us (1%)
  local copies, waits for them, and re-layouts  0.91 us (1%)
    all_to_all x1, blocking collectives, body(): lax.all_to_all(attended, 'head', split_axis=0, concat_axis=1, tiled=True)  29.1 us
    all_to_all x1, starting transfers between devices, body(): mine = lax.all_to_all(sent, 'ctx', 0, 0, axis_index_groups=GROUPS_XY)  11.3 us
    pallas_call x1, Pallas kernels, attention(): pl.pallas_call(functools.partial(attention_kernel, heads), out_shape=[jax...  7.92 us
    ppermute x3, waiting for transfers between devices, body(): lax.ppermute(anchor, 'ctx', pairs)  6.98 us
    ppermute x2, waiting for transfers between devices, body(): anchor = anchor + lax.ppermute(anchor, 'ctx', pairs)  3.77 us
    ppermute x1, starting transfers between devices, body(): anchors = [anchor, lax.ppermute(anchor, 'ctx', PAIRS_Y[2])]  3.71 us
    ppermute x3, starting transfers between devices, body(): lax.ppermute(anchor, 'ctx', pairs)  2.62 us
    ppermute x2, starting transfers between devices, body(): anchor = anchor + lax.ppermute(anchor, 'ctx', pairs)  2.59 us
  transfers between devices with their start and end apart: 9, of which 3 were waited for; matrix products, arithmetic and copies ran while one was open for 1% of the time, Pallas kernels for 10%

profile of v4, /device:TPU:6, one launch (start us, length us, event | category | flops | bytes accessed | tf_op | source)
XLA Modules:
  0.0 76.0 jit_solution(799040448279929045)
XLA Ops:
  0.0 0.0 copy-start.1
  0.0 0.0 copy-start.2
  0.0 0.0 copy-start
  0.0 2.1 %shard_map.46 = (bf16[32,64,128]{2,1,0:T(8,128)(2,1)}, bf16[256,128]{1,0:T(8,128)(2,1)}) custom-call(s32[1,32]{1,0:T(1,128)} %kept_ref.1, bf16[512,128]{1,0:T(8,128)(2,1)} %key_ref.3, bf16[512,128]{1,0:T(8,128)(2,1)} %value_ref.3), custom_call_target="tpu_custom_call" | custom-call | tf_op jit(solution)/shard_map/pallas_call | solution.py:57
  2.1 0.7 collective-permute-start
  2.8 0.0 collective-permute-done
  2.8 11.3 %all-to-all-start = ((bf16[32,64,128]{2,1,0:T(8,128)(2,1)}), bf16[32,64,128]{2,1,0:T(8,128)(2,1)S(1)}, u32[]{:S(2)}, u32[]{:S(2)}) async-start(bf16[32,64,128]{2,1,0:T(8,128)(2,1)} %get-tuple-element.15), calls=%async_computation | async-start | bytes 1048576 | tf_op jit(solution)/shard_map/all_to_all | solution.py:199
  14.1 0.9 %add.18 = bf16[256,128]{1,0:T(8,128)(2,1)S(1)} add(bf16[256,128]{1,0:T(8,128)(2,1)} %get-tuple-element.14, bf16[256,128]{1,0:T(8,128)(2,1)S(1)} %collective-permute-done) | non-fusion elementwise | flops 32768 | bytes 196608 | tf_op jit(solution)/shard_map/add | solution.py:200
  14.9 0.7 collective-permute-start.1
  15.6 0.7 collective-permute-start.2
  16.3 1.3 %collective-permute-start.3 = (bf16[256,128]{1,0:T(8,128)(2,1)S(1)}, bf16[256,128]{1,0:T(8,128)(2,1)S(1)}, u32[]{:S(2)}, u32[]{:S(2)}) collective-permute-start(bf16[256,128]{1,0:T(8,128)(2,1)S(1)} %add.18), channel_id=1, source_target_pairs={{0,384},{8,392},{1,385},{9,393},{2,386},{10,394},{3,387},{11,395},... | collective-permute-start | bytes 196616 | tf_op jit(solution)/shard_map/ppermute | solution.py:201
  17.6 0.0 collective-permute-done.1
  17.6 0.0 collective-permute-done.2
  17.6 7.0 %collective-permute-done.3 = bf16[256,128]{1,0:T(8,128)(2,1)S(1)} collective-permute-done((bf16[256,128]{1,0:T(8,128)(2,1)S(1)}, bf16[256,128]{1,0:T(8,128)(2,1)S(1)}, u32[]{:S(2)}, u32[]{:S(2)}) %collective-permute-start.3) | collective-permute-done | bytes 65568 | tf_op jit(solution)/shard_map/ppermute | solution.py:201
  24.6 1.3 %collective-permute-start.4 = (bf16[256,128]{1,0:T(8,128)(2,1)S(1)}, bf16[256,128]{1,0:T(8,128)(2,1)S(1)}, u32[]{:S(2)}, u32[]{:S(2)}) collective-permute-start(bf16[256,128]{1,0:T(8,128)(2,1)S(1)} %add_add_fusion), channel_id=1, source_target_pairs={{0,96},{8,104},{128,224},{136,232},{256,352},{264,360},{384,480},{... | collective-permute-start | bytes 196616 | tf_op jit(solution)/shard_map/ppermute | solution.py:203
  25.9 1.9 %collective-permute-done.4 = bf16[256,128]{1,0:T(8,128)(2,1)S(1)} collective-permute-done((bf16[256,128]{1,0:T(8,128)(2,1)S(1)}, bf16[256,128]{1,0:T(8,128)(2,1)S(1)}, u32[]{:S(2)}, u32[]{:S(2)}) %collective-permute-start.4) | collective-permute-done | bytes 65568 | tf_op jit(solution)/shard_map/ppermute | solution.py:203
  27.8 1.3 %collective-permute-start.5 = (bf16[256,128]{1,0:T(8,128)(2,1)S(1)}, bf16[256,128]{1,0:T(8,128)(2,1)S(1)}, u32[]{:S(2)}, u32[]{:S(2)}) collective-permute-start(bf16[256,128]{1,0:T(8,128)(2,1)S(1)} %add.22), channel_id=1, source_target_pairs={{0,32},{8,40},{96,64},{104,72},{128,160},{136,168},{224,192},{232,... | collective-permute-start | bytes 196616 | tf_op jit(solution)/shard_map/ppermute | solution.py:203
  29.1 1.9 %collective-permute-done.5 = bf16[256,128]{1,0:T(8,128)(2,1)S(1)} collective-permute-done((bf16[256,128]{1,0:T(8,128)(2,1)S(1)}, bf16[256,128]{1,0:T(8,128)(2,1)S(1)}, u32[]{:S(2)}, u32[]{:S(2)}) %collective-permute-start.5) | collective-permute-done | bytes 65568 | tf_op jit(solution)/shard_map/ppermute | solution.py:203
  31.0 0.0 all-to-all-done.mine_ref
  31.0 1.9 %collective-permute-start.6 = (bf16[32,64,128]{2,1,0:T(8,128)(2,1)S(1)}, bf16[32,64,128]{2,1,0:T(8,128)(2,1)S(1)}, u32[]{:S(2)}, u32[]{:S(2)}) collective-permute-start(bf16[32,64,128]{2,1,0:T(8,128)(2,1)S(1)} %all-to-all-done.mine_ref), channel_id=1, source_target_pairs={{0,8},{8,0},{16,24},{24,16},{32,40},{40,32},{48,56},{56,48},{64,72... | collective-permute-start | bytes 1572872 | tf_op jit(solution)/shard_map/ppermute | solution.py:206
  32.9 3.7 %collective-permute-start.7 = (bf16[256,128]{1,0:T(8,128)(2,1)S(1)}, bf16[256,128]{1,0:T(8,128)(2,1)S(1)}, u32[]{:S(2)}, u32[]{:S(2)}) collective-permute-start(bf16[256,128]{1,0:T(8,128)(2,1)S(1)} %add.23.refs_0_), channel_id=1, source_target_pairs={{0,16},{8,24},{32,48},{40,56},{64,80},{72,88},{96,112},{104,120},{... | collective-permute-start | bytes 196616 | tf_op jit(solution)/shard_map/ppermute | solution.py:205
  36.7 0.0 collective-permute-done.6.other_ref
  36.7 0.0 copy-done.1
  36.7 0.0 copy-done.2
  36.7 0.0 copy-done
  36.7 7.9 %shard_map.47 = (f32[512,640]{1,0:T(8,128)S(1)}, f32[512,640]{1,0:T(8,128)S(1)}) custom-call(bf16[512,640]{1,0:T(8,128)(2,1)S(1)} %copy-done, bf16[32,64,128]{2,1,0:T(8,128)(2,1)S(1)} %all-to-all-done.mine_ref, bf16[32,64,128]{2,1,0:T(8,128)(2,1)S(1)} %collective-permute-done.6.other_ref, bf16[512,128]{1,0:T(8,128)(2,1)S(1)} %copy-done.1, ...), custom_call_target="tpu_custom_call" | custom-call | tf_op jit(solution)/shard_map/pallas_call | solution.py:146
  44.6 0.0 collective-permute-done.7.refs_1_
  44.6 1.4 %shard_map.48 = bf16[512,640]{1,0:T(8,128)(2,1)S(1)} custom-call(bf16[512,640]{1,0:T(8,128)(2,1)S(1)} %copy-done, f32[512,640]{1,0:T(8,128)S(1)} %get-tuple-element.18.part_ref, f32[512,640]{1,0:T(8,128)S(1)} %get-tuple-element.19.log_ref, bf16[256,128]{1,0:T(8,128)(2,1)S(1)} %add.23.refs_0_, bf16[256,128]{1,0:T(8,128)(2,1)S(1)} %collective-permute-done.7.refs_1_), custom_call_target="tpu_custom_call" | custom-call | tf_op jit(solution)/shard_map/pallas_call | solution.py:188
  46.0 29.1 %all_to_all.24 = bf16[8,64,640]{2,1,0:T(8,128)(2,1)S(1)} all-to-all(bf16[8,64,640]{2,1,0:T(8,128)(2,1)S(1)} %bitcast.4), channel_id=1, replica_groups=mesh['ctx'=64,'head'=8] {'head'}, dimensions={0} | all-to-all | bytes 1310720 | tf_op jit(solution)/shard_map/all_to_all | solution.py:210
  75.1 0.9 %copy.6 = bf16[8,8,8,640]{3,2,0,1:T(8,128)(2,1)} copy(bf16[8,8,8,640]{3,2,1,0:T(8,128)(2,1)S(1)} %bitcast.5) | data formatting | bytes 1310720 | tf_op jit(solution)/shard_map/all_to_all | solution.py:210
  (3 shorter events, 0.1 us)
Async XLA Ops:
  0.0 36.7 %copy-start.1 = (bf16[512,128]{1,0:T(8,128)(2,1)S(1)}, bf16[512,128]{1,0:T(8,128)(2,1)}, u32[]{:S(2)}) copy-start(bf16[512,128]{1,0:T(8,128)(2,1)} %key_ref.3) | copy-start | bytes 393220
  0.0 36.7 %copy-start.2 = (bf16[512,128]{1,0:T(8,128)(2,1)S(1)}, bf16[512,128]{1,0:T(8,128)(2,1)}, u32[]{:S(2)}) copy-start(bf16[512,128]{1,0:T(8,128)(2,1)} %value_ref.3) | copy-start | bytes 393220
  0.0 36.7 %copy-start = (bf16[512,640]{1,0:T(8,128)(2,1)S(1)}, bf16[512,640]{1,0:T(8,128)(2,1)}, u32[]{:S(2)}) copy-start(bf16[512,640]{1,0:T(8,128)(2,1)} %q_ref.3) | copy-start | bytes 1966084
  2.1 0.7 collective-permute-start
  2.8 28.2 %all-to-all-start = ((bf16[32,64,128]{2,1,0:T(8,128)(2,1)}), bf16[32,64,128]{2,1,0:T(8,128)(2,1)S(1)}, u32[]{:S(2)}, u32[]{:S(2)}) async-start(bf16[32,64,128]{2,1,0:T(8,128)(2,1)} %get-tuple-element.15), calls=%async_computation | async-start | bytes 1048576 | tf_op jit(solution)/shard_map/all_to_all | solution.py:199
  14.9 2.6 %collective-permute-start.1 = (bf16[256,128]{1,0:T(8,128)(2,1)S(1)}, bf16[256,128]{1,0:T(8,128)(2,1)S(1)}, u32[]{:S(2)}, u32[]{:S(2)}) collective-permute-start(bf16[256,128]{1,0:T(8,128)(2,1)S(1)} %add.18), channel_id=1, source_target_pairs={{0,128},{8,136},{1,129},{9,137},{2,130},{10,138},{3,131},{11,139},... | collective-permute-start | bytes 196616 | tf_op jit(solution)/shard_map/ppermute | solution.py:201
  15.6 2.0 %collective-permute-start.2 = (bf16[256,128]{1,0:T(8,128)(2,1)S(1)}, bf16[256,128]{1,0:T(8,128)(2,1)S(1)}, u32[]{:S(2)}, u32[]{:S(2)}) collective-permute-start(bf16[256,128]{1,0:T(8,128)(2,1)S(1)} %add.18), channel_id=1, source_target_pairs={{0,256},{8,264},{1,257},{9,265},{2,258},{10,266},{3,259},{11,267},... | collective-permute-start | bytes 196616 | tf_op jit(solution)/shard_map/ppermute | solution.py:201
  16.3 8.3 %collective-permute-start.3 = (bf16[256,128]{1,0:T(8,128)(2,1)S(1)}, bf16[256,128]{1,0:T(8,128)(2,1)S(1)}, u32[]{:S(2)}, u32[]{:S(2)}) collective-permute-start(bf16[256,128]{1,0:T(8,128)(2,1)S(1)} %add.18), channel_id=1, source_target_pairs={{0,384},{8,392},{1,385},{9,393},{2,386},{10,394},{3,387},{11,395},... | collective-permute-start | bytes 196616 | tf_op jit(solution)/shard_map/ppermute | solution.py:201
  24.6 3.2 %collective-permute-start.4 = (bf16[256,128]{1,0:T(8,128)(2,1)S(1)}, bf16[256,128]{1,0:T(8,128)(2,1)S(1)}, u32[]{:S(2)}, u32[]{:S(2)}) collective-permute-start(bf16[256,128]{1,0:T(8,128)(2,1)S(1)} %add_add_fusion), channel_id=1, source_target_pairs={{0,96},{8,104},{128,224},{136,232},{256,352},{264,360},{384,480},{... | collective-permute-start | bytes 196616 | tf_op jit(solution)/shard_map/ppermute | solution.py:203
  27.8 3.2 %collective-permute-start.5 = (bf16[256,128]{1,0:T(8,128)(2,1)S(1)}, bf16[256,128]{1,0:T(8,128)(2,1)S(1)}, u32[]{:S(2)}, u32[]{:S(2)}) collective-permute-start(bf16[256,128]{1,0:T(8,128)(2,1)S(1)} %add.22), channel_id=1, source_target_pairs={{0,32},{8,40},{96,64},{104,72},{128,160},{136,168},{224,192},{232,... | collective-permute-start | bytes 196616 | tf_op jit(solution)/shard_map/ppermute | solution.py:203
  31.0 5.7 %collective-permute-start.6 = (bf16[32,64,128]{2,1,0:T(8,128)(2,1)S(1)}, bf16[32,64,128]{2,1,0:T(8,128)(2,1)S(1)}, u32[]{:S(2)}, u32[]{:S(2)}) collective-permute-start(bf16[32,64,128]{2,1,0:T(8,128)(2,1)S(1)} %all-to-all-done.mine_ref), channel_id=1, source_target_pairs={{0,8},{8,0},{16,24},{24,16},{32,40},{40,32},{48,56},{56,48},{64,72... | collective-permute-start | bytes 1572872 | tf_op jit(solution)/shard_map/ppermute | solution.py:206
  32.9 11.7 %collective-permute-start.7 = (bf16[256,128]{1,0:T(8,128)(2,1)S(1)}, bf16[256,128]{1,0:T(8,128)(2,1)S(1)}, u32[]{:S(2)}, u32[]{:S(2)}) collective-permute-start(bf16[256,128]{1,0:T(8,128)(2,1)S(1)} %add.23.refs_0_), channel_id=1, source_target_pairs={{0,16},{8,24},{32,48},{40,56},{64,80},{72,88},{96,112},{104,120},{... | collective-permute-start | bytes 196616 | tf_op jit(solution)/shard_map/ppermute | solution.py:205

commit v5 on v3

--- a/solution.py
+++ b/solution.py
@@ -28,7 +28,7 @@
 
 GROUPS_XY = [[ctx_of(x, y, c) for x in range(NX) for y in range(NY)] for c in range(NC)]
 PAIRS_UP = [(0, 1)]
-PAIRS_X = [[(c, ctx_of(x, 0, c)) for c in range(NC)] for x in range(1, NX)]
+PAIRS_X = [[(c, ctx_of(x, 0, c)) for c in range(NC)] for x in (3, 2, 1)]
 PAIRS_Y = [
     [(ctx_of(x, y, c), ctx_of(x, to, c)) for x in range(NX) for y, to in hops for c in range(NC)]
     for hops in ([(0, 6)], [(0, 2), (6, 4)], [(0, 1), (2, 3), (4, 5), (6, 7)])
@@ -61,31 +61,40 @@
     )(kept, keys, values)
 
 
-def attention_kernel(
-    heads, q_ref, mine_ref, other_ref, key_ref, value_ref, out_ref, log_ref,
+def attention_kernel(heads, *refs):
+    for x in range(NX):
+        pl.when(lax.axis_index("ctx") // (NY * NC) == x)(
+            functools.partial(attend, heads, (x + 1) * NY, *refs)
+        )
+
+
+def attend(
+    heads, chips, q_ref, mine_ref, other_ref, key_ref, value_ref, out_ref, log_ref,
     kx, kt, vx, s0, s1, p0, p1, m0, m1,
 ):
     me = lax.axis_index("ctx")
     core = lax.rem(me, NC)
-
-    for ref, base in ((mine_ref, 0), (other_ref, HALF)):
-        for chip in range(CHIPS):
+    half = chips * PASS
+    far = 2 * half
+
+    for ref, base in ((mine_ref, 0), (other_ref, half)):
+        for chip in range(chips):
             at = slice(base + chip * PASS, base + (chip + 1) * PASS)
             kx[at, :] = ref[chip, :PASS, :]
             vx[at, :HD] = ref[chip, PASS:, :]
-    kx[FAR:, :] = key_ref[...]
-    vx[FAR:, :HD] = value_ref[...]
-    vx[:, HD:] = jnp.ones((FAR + ROWS, HD), jnp.bfloat16)
-
-    for start in range(0, FAR + ROWS, HD):
+    kx[far : far + ROWS, :] = key_ref[...]
+    vx[far : far + ROWS, :HD] = value_ref[...]
+    vx[: far + ROWS, HD:] = jnp.ones((far + ROWS, HD), jnp.bfloat16)
+
+    for start in range(0, far + ROWS, HD):
         kt[:HD, start : start + HD] = kx[start : start + HD, :].T
-    row = lax.broadcasted_iota(jnp.int32, (HD, HALF), 0)
-    at = lax.broadcasted_iota(jnp.int32, (HD, HALF), 1)
+    row = lax.broadcasted_iota(jnp.int32, (HD, half), 0)
+    at = lax.broadcasted_iota(jnp.int32, (HD, half), 1)
     never = jnp.where(row == 0, NEG, 0.0)
-    for owner_core, base in ((core, 0), (1 - core, HALF)):
+    for owner_core, base in ((core, 0), (1 - core, half)):
         owner = NC * (at >> 5) + owner_core
-        kt[HD:, base : base + HALF] = jnp.where(owner < me, 0.0, never).astype(jnp.bfloat16)
-    kt[HD:, FAR:] = jnp.zeros((HD, ROWS), jnp.bfloat16)
+        kt[HD:, base : base + half] = jnp.where(owner < me, 0.0, never).astype(jnp.bfloat16)
+    kt[HD:, far : far + ROWS] = jnp.zeros((HD, ROWS), jnp.bfloat16)
 
     lane = lax.broadcasted_iota(jnp.int32, (TILE, HD), 1)
     flag = jnp.where(lane == 0, 1.0, 0.0).astype(jnp.bfloat16)
@@ -97,10 +106,10 @@
     )
 
     def width(tile):
-        return FAR + (tile + 1) * TILE
+        return far + (tile + 1) * TILE
 
     def pieces(index):
-        cuts = [*range(0, FAR, TILE), *range(FAR, width(items[index][1]) + 1, TILE)]
+        cuts = [*range(0, far, TILE), *range(far, width(items[index][1]) + 1, TILE)]
         return [(index, start, stop) for start, stop in zip(cuts[:-1], cuts[1:])]
 
     def score(index, start, stop):

time: 77.1 us -> 75.9 us (0.984); the launches traced: 75.6 us -> 75.5 us
    ppermute x3, waiting for transfers between devices: 6.98 us -> 6.03 us  [body(): lax.ppermute(anchor, 'ctx', pairs)]
where the time goes in v5:
time: 75.9 us; the launch traced here: 75.5 us
  blocking collectives  29 us (38%)
  starting transfers between devices  22.8 us (30%)
  Pallas kernels  11.4 us (15%)
  waiting for transfers between devices  10.3 us (14%)
  other arithmetic  0.92 us (1%)
  local copies, waits for them, and re-layouts  0.91 us (1%)
    all_to_all x1, blocking collectives, body(): lax.all_to_all(attended, 'head', split_axis=0, concat_axis=1, tiled=True)  29 us
    all_to_all x1, starting transfers between devices, body(): mine = lax.all_to_all(sent, 'ctx', 0, 0, axis_index_groups=GROUPS_XY)  11.3 us
    pallas_call x1, Pallas kernels, attention(): pl.pallas_call(functools.partial(attention_kernel, heads), out_shape=[jax...  7.87 us
    ppermute x3, waiting for transfers between devices, body(): lax.ppermute(anchor, 'ctx', pairs)  6.03 us
    ppermute x2, waiting for transfers between devices, body(): anchor = anchor + lax.ppermute(anchor, 'ctx', pairs)  4.26 us
    ppermute x1, starting transfers between devices, body(): anchors = [anchor, lax.ppermute(anchor, 'ctx', PAIRS_Y[2])]  3.73 us
    ppermute x3, starting transfers between devices, body(): lax.ppermute(anchor, 'ctx', pairs)  2.62 us
    ppermute x2, starting transfers between devices, body(): anchor = anchor + lax.ppermute(anchor, 'ctx', pairs)  2.59 us
  transfers between devices with their start and end apart: 9, of which 3 were waited for; matrix products, arithmetic and copies ran while one was open for 1% of the time, Pallas kernels for 10%

profile of v5, /device:TPU:6, one launch (start us, length us, event | category | flops | bytes accessed | tf_op | source)
XLA Modules:
  0.0 75.5 jit_solution(14021593272636987967)
XLA Ops:
  0.0 0.0 copy-start.1
  0.0 0.0 copy-start.2
  0.0 0.0 copy-start
  0.0 2.1 %shard_map.46 = (bf16[32,64,128]{2,1,0:T(8,128)(2,1)}, bf16[256,128]{1,0:T(8,128)(2,1)}) custom-call(s32[1,32]{1,0:T(1,128)} %kept_ref.1, bf16[512,128]{1,0:T(8,128)(2,1)} %refs_3_.1, bf16[512,128]{1,0:T(8,128)(2,1)} %refs_4_.1), custom_call_target="tpu_custom_call" | custom-call | tf_op jit(solution)/shard_map/pallas_call | solution.py:55
  2.1 0.7 collective-permute-start
  2.8 0.0 collective-permute-done
  2.8 11.3 %all-to-all-start = ((bf16[32,64,128]{2,1,0:T(8,128)(2,1)}), bf16[32,64,128]{2,1,0:T(8,128)(2,1)S(1)}, u32[]{:S(2)}, u32[]{:S(2)}) async-start(bf16[32,64,128]{2,1,0:T(8,128)(2,1)} %get-tuple-element.15), calls=%async_computation | async-start | bytes 1048576 | tf_op jit(solution)/shard_map/all_to_all | solution.py:206
  14.1 0.9 %add.18 = bf16[256,128]{1,0:T(8,128)(2,1)S(1)} add(bf16[256,128]{1,0:T(8,128)(2,1)} %get-tuple-element.14, bf16[256,128]{1,0:T(8,128)(2,1)S(1)} %collective-permute-done) | non-fusion elementwise | flops 32768 | bytes 196608 | tf_op jit(solution)/shard_map/add | solution.py:207
  14.9 1.3 %collective-permute-start.1 = (bf16[256,128]{1,0:T(8,128)(2,1)S(1)}, bf16[256,128]{1,0:T(8,128)(2,1)S(1)}, u32[]{:S(2)}, u32[]{:S(2)}) collective-permute-start(bf16[256,128]{1,0:T(8,128)(2,1)S(1)} %add.18), channel_id=1, source_target_pairs={{0,384},{8,392},{1,385},{9,393},{2,386},{10,394},{3,387},{11,395},... | collective-permute-start | bytes 196616 | tf_op jit(solution)/shard_map/ppermute | solution.py:208
  16.2 0.7 collective-permute-start.2
  16.9 0.7 collective-permute-start.3
  17.6 6.0 %collective-permute-done.1 = bf16[256,128]{1,0:T(8,128)(2,1)S(1)} collective-permute-done((bf16[256,128]{1,0:T(8,128)(2,1)S(1)}, bf16[256,128]{1,0:T(8,128)(2,1)S(1)}, u32[]{:S(2)}, u32[]{:S(2)}) %collective-permute-start.1) | collective-permute-done | bytes 65568 | tf_op jit(solution)/shard_map/ppermute | solution.py:208
  23.6 0.0 collective-permute-done.2
  23.6 0.0 collective-permute-done.3
  23.6 1.3 %collective-permute-start.4 = (bf16[256,128]{1,0:T(8,128)(2,1)S(1)}, bf16[256,128]{1,0:T(8,128)(2,1)S(1)}, u32[]{:S(2)}, u32[]{:S(2)}) collective-permute-start(bf16[256,128]{1,0:T(8,128)(2,1)S(1)} %add_add_fusion), channel_id=1, source_target_pairs={{0,96},{8,104},{128,224},{136,232},{256,352},{264,360},{384,480},{... | collective-permute-start | bytes 196616 | tf_op jit(solution)/shard_map/ppermute | solution.py:210
  24.9 2.4 %collective-permute-done.4 = bf16[256,128]{1,0:T(8,128)(2,1)S(1)} collective-permute-done((bf16[256,128]{1,0:T(8,128)(2,1)S(1)}, bf16[256,128]{1,0:T(8,128)(2,1)S(1)}, u32[]{:S(2)}, u32[]{:S(2)}) %collective-permute-start.4) | collective-permute-done | bytes 65568 | tf_op jit(solution)/shard_map/ppermute | solution.py:210
  27.3 1.3 %collective-permute-start.5 = (bf16[256,128]{1,0:T(8,128)(2,1)S(1)}, bf16[256,128]{1,0:T(8,128)(2,1)S(1)}, u32[]{:S(2)}, u32[]{:S(2)}) collective-permute-start(bf16[256,128]{1,0:T(8,128)(2,1)S(1)} %add.22), channel_id=1, source_target_pairs={{0,32},{8,40},{96,64},{104,72},{128,160},{136,168},{224,192},{232,... | collective-permute-start | bytes 196616 | tf_op jit(solution)/shard_map/ppermute | solution.py:210
  28.6 1.9 %collective-permute-done.5 = bf16[256,128]{1,0:T(8,128)(2,1)S(1)} collective-permute-done((bf16[256,128]{1,0:T(8,128)(2,1)S(1)}, bf16[256,128]{1,0:T(8,128)(2,1)S(1)}, u32[]{:S(2)}, u32[]{:S(2)}) %collective-permute-start.5) | collective-permute-done | bytes 65568 | tf_op jit(solution)/shard_map/ppermute | solution.py:210
  30.5 0.0 all-to-all-done.refs_1_
  30.5 1.9 %collective-permute-start.6 = (bf16[32,64,128]{2,1,0:T(8,128)(2,1)S(1)}, bf16[32,64,128]{2,1,0:T(8,128)(2,1)S(1)}, u32[]{:S(2)}, u32[]{:S(2)}) collective-permute-start(bf16[32,64,128]{2,1,0:T(8,128)(2,1)S(1)} %all-to-all-done.refs_1_), channel_id=1, source_target_pairs={{0,8},{8,0},{16,24},{24,16},{32,40},{40,32},{48,56},{56,48},{64,72... | collective-permute-start | bytes 1572872 | tf_op jit(solution)/shard_map/ppermute | solution.py:213
  32.5 3.7 %collective-permute-start.7 = (bf16[256,128]{1,0:T(8,128)(2,1)S(1)}, bf16[256,128]{1,0:T(8,128)(2,1)S(1)}, u32[]{:S(2)}, u32[]{:S(2)}) collective-permute-start(bf16[256,128]{1,0:T(8,128)(2,1)S(1)} %add.23.refs_0_), channel_id=1, source_target_pairs={{0,16},{8,24},{32,48},{40,56},{64,80},{72,88},{96,112},{104,120},{... | collective-permute-start | bytes 196616 | tf_op jit(solution)/shard_map/ppermute | solution.py:212
  36.2 0.0 collective-permute-done.6.refs_2_
  36.2 0.0 copy-done.1
  36.2 0.0 copy-done.2
  36.2 0.0 copy-done
  36.3 7.9 %shard_map.47 = (f32[512,640]{1,0:T(8,128)S(1)}, f32[512,640]{1,0:T(8,128)S(1)}) custom-call(bf16[512,640]{1,0:T(8,128)(2,1)S(1)} %copy-done, bf16[32,64,128]{2,1,0:T(8,128)(2,1)S(1)} %all-to-all-done.refs_1_, bf16[32,64,128]{2,1,0:T(8,128)(2,1)S(1)} %collective-permute-done.6.refs_2_, bf16[512,128]{1,0:T(8,128)(2,1)S(1)} %copy-done.1, ...), custom_call_target="tpu_custom_call" | custom-call | tf_op jit(solution)/shard_map/pallas_call | solution.py:153
  44.1 0.0 collective-permute-done.7.refs_1_
  44.1 1.4 %shard_map.48 = bf16[512,640]{1,0:T(8,128)(2,1)S(1)} custom-call(bf16[512,640]{1,0:T(8,128)(2,1)S(1)} %copy-done, f32[512,640]{1,0:T(8,128)S(1)} %get-tuple-element.18.part_ref, f32[512,640]{1,0:T(8,128)S(1)} %get-tuple-element.19.log_ref, bf16[256,128]{1,0:T(8,128)(2,1)S(1)} %add.23.refs_0_, bf16[256,128]{1,0:T(8,128)(2,1)S(1)} %collective-permute-done.7.refs_1_), custom_call_target="tpu_custom_call" | custom-call | tf_op jit(solution)/shard_map/pallas_call | solution.py:195
  45.5 29.0 %all_to_all.24 = bf16[8,64,640]{2,1,0:T(8,128)(2,1)S(1)} all-to-all(bf16[8,64,640]{2,1,0:T(8,128)(2,1)S(1)} %bitcast.4), channel_id=1, replica_groups=mesh['ctx'=64,'head'=8] {'head'}, dimensions={0} | all-to-all | bytes 1310720 | tf_op jit(solution)/shard_map/all_to_all | solution.py:217
  74.6 0.9 %copy.6 = bf16[8,8,8,640]{3,2,0,1:T(8,128)(2,1)} copy(bf16[8,8,8,640]{3,2,1,0:T(8,128)(2,1)S(1)} %bitcast.5) | data formatting | bytes 1310720 | tf_op jit(solution)/shard_map/all_to_all | solution.py:217
  (3 shorter events, 0.1 us)
Async XLA Ops:
  0.0 36.2 %copy-start.1 = (bf16[512,128]{1,0:T(8,128)(2,1)S(1)}, bf16[512,128]{1,0:T(8,128)(2,1)}, u32[]{:S(2)}) copy-start(bf16[512,128]{1,0:T(8,128)(2,1)} %refs_3_.1) | copy-start | bytes 393220
  0.0 36.2 %copy-start.2 = (bf16[512,128]{1,0:T(8,128)(2,1)S(1)}, bf16[512,128]{1,0:T(8,128)(2,1)}, u32[]{:S(2)}) copy-start(bf16[512,128]{1,0:T(8,128)(2,1)} %refs_4_.1) | copy-start | bytes 393220
  0.0 36.2 %copy-start = (bf16[512,640]{1,0:T(8,128)(2,1)S(1)}, bf16[512,640]{1,0:T(8,128)(2,1)}, u32[]{:S(2)}) copy-start(bf16[512,640]{1,0:T(8,128)(2,1)} %q_ref.1) | copy-start | bytes 1966084
  2.1 0.7 collective-permute-start
  2.8 27.7 %all-to-all-start = ((bf16[32,64,128]{2,1,0:T(8,128)(2,1)}), bf16[32,64,128]{2,1,0:T(8,128)(2,1)S(1)}, u32[]{:S(2)}, u32[]{:S(2)}) async-start(bf16[32,64,128]{2,1,0:T(8,128)(2,1)} %get-tuple-element.15), calls=%async_computation | async-start | bytes 1048576 | tf_op jit(solution)/shard_map/all_to_all | solution.py:206
  14.9 8.7 %collective-permute-start.1 = (bf16[256,128]{1,0:T(8,128)(2,1)S(1)}, bf16[256,128]{1,0:T(8,128)(2,1)S(1)}, u32[]{:S(2)}, u32[]{:S(2)}) collective-permute-start(bf16[256,128]{1,0:T(8,128)(2,1)S(1)} %add.18), channel_id=1, source_target_pairs={{0,384},{8,392},{1,385},{9,393},{2,386},{10,394},{3,387},{11,395},... | collective-permute-start | bytes 196616 | tf_op jit(solution)/shard_map/ppermute | solution.py:208
  16.2 7.4 %collective-permute-start.2 = (bf16[256,128]{1,0:T(8,128)(2,1)S(1)}, bf16[256,128]{1,0:T(8,128)(2,1)S(1)}, u32[]{:S(2)}, u32[]{:S(2)}) collective-permute-start(bf16[256,128]{1,0:T(8,128)(2,1)S(1)} %add.18), channel_id=1, source_target_pairs={{0,256},{8,264},{1,257},{9,265},{2,258},{10,266},{3,259},{11,267},... | collective-permute-start | bytes 196616 | tf_op jit(solution)/shard_map/ppermute | solution.py:208
  16.9 6.7 %collective-permute-start.3 = (bf16[256,128]{1,0:T(8,128)(2,1)S(1)}, bf16[256,128]{1,0:T(8,128)(2,1)S(1)}, u32[]{:S(2)}, u32[]{:S(2)}) collective-permute-start(bf16[256,128]{1,0:T(8,128)(2,1)S(1)} %add.18), channel_id=1, source_target_pairs={{0,128},{8,136},{1,129},{9,137},{2,130},{10,138},{3,131},{11,139},... | collective-permute-start | bytes 196616 | tf_op jit(solution)/shard_map/ppermute | solution.py:208
  23.6 3.7 %collective-permute-start.4 = (bf16[256,128]{1,0:T(8,128)(2,1)S(1)}, bf16[256,128]{1,0:T(8,128)(2,1)S(1)}, u32[]{:S(2)}, u32[]{:S(2)}) collective-permute-start(bf16[256,128]{1,0:T(8,128)(2,1)S(1)} %add_add_fusion), channel_id=1, source_target_pairs={{0,96},{8,104},{128,224},{136,232},{256,352},{264,360},{384,480},{... | collective-permute-start | bytes 196616 | tf_op jit(solution)/shard_map/ppermute | solution.py:210
  27.3 3.2 %collective-permute-start.5 = (bf16[256,128]{1,0:T(8,128)(2,1)S(1)}, bf16[256,128]{1,0:T(8,128)(2,1)S(1)}, u32[]{:S(2)}, u32[]{:S(2)}) collective-permute-start(bf16[256,128]{1,0:T(8,128)(2,1)S(1)} %add.22), channel_id=1, source_target_pairs={{0,32},{8,40},{96,64},{104,72},{128,160},{136,168},{224,192},{232,... | collective-permute-start | bytes 196616 | tf_op jit(solution)/shard_map/ppermute | solution.py:210
  30.5 5.7 %collective-permute-start.6 = (bf16[32,64,128]{2,1,0:T(8,128)(2,1)S(1)}, bf16[32,64,128]{2,1,0:T(8,128)(2,1)S(1)}, u32[]{:S(2)}, u32[]{:S(2)}) collective-permute-start(bf16[32,64,128]{2,1,0:T(8,128)(2,1)S(1)} %all-to-all-done.refs_1_), channel_id=1, source_target_pairs={{0,8},{8,0},{16,24},{24,16},{32,40},{40,32},{48,56},{56,48},{64,72... | collective-permute-start | bytes 1572872 | tf_op jit(solution)/shard_map/ppermute | solution.py:213
  32.5 11.7 %collective-permute-start.7 = (bf16[256,128]{1,0:T(8,128)(2,1)S(1)}, bf16[256,128]{1,0:T(8,128)(2,1)S(1)}, u32[]{:S(2)}, u32[]{:S(2)}) collective-permute-start(bf16[256,128]{1,0:T(8,128)(2,1)S(1)} %add.23.refs_0_), channel_id=1, source_target_pairs={{0,16},{8,24},{32,48},{40,56},{64,80},{72,88},{96,112},{104,120},{... | collective-permute-start | bytes 196616 | tf_op jit(solution)/shard_map/ppermute | solution.py:212
